TPU v7x, 32 devices: a whole 2x2x4 slice. The times are simulated.
32 devices in a mesh: patch: 8 (over y, x, core), head: 4 (over z).
Axes of the slice: x: 2, y: 2, z: 4, core: 2. Of those that a mesh axis runs over, the one named last changes fastest.
Arguments:
- patches: bfloat16 [2, 512, 9216], P(None, 'head', 'patch'), may hold values from -8 to 8
- hole_mask: int32 [2, 9216], P(None, 'patch'), may hold values from 0 to 1, as said below
- seg_start: int32 [2, 256], replicated, may hold values from 0 to 9215, as said below
- cotangent: bfloat16 [2, 512, 9216], P(None, 'head', 'patch'), may hold values from -6 to 6
- qkv_weight: float32 [1536, 512], P('head'), may hold values from -0.375 to 0.375
- out_weight: float32 [512, 512], P('head'), may hold values from -0.25 to 0.25
- norm_params: float32 [2, 512], replicated, may hold values from -1.2 to 1.8, as said below
- biases: float32 [4, 512], P(None, 'head'), may hold values from -1.5 to 1.5
- kernels: float32 [83, 512], P(None, 'head'), may hold values from -0.5 to 0.5
- conv_weight: float32 [8, 33], P('head'), may hold values from -1 to 1
- qkv_rows: float32 [1536], P('head'), may hold values from 1843.2 to 27648
- qkv_cols: float32 [512], replicated, may hold values from 1843.2 to 27648
- out_rows: float32 [512], P('head'), may hold values from 9216 to 147456
- out_cols: float32 [512], replicated, may hold values from 9216 to 147456
- norm_second: float32 [2, 512], replicated, may hold values from 9216 to 147456
- bias_second: float32 [4, 512], P(None, 'head'), may hold values from 2764.8 to 40550.4
- kernel_second: float32 [83, 512], P(None, 'head'), may hold values from 9216 to 129024
- conv_second: float32 [8, 33], P('head'), may hold values from 460800 to 7004160
Outputs:
- block_out: bfloat16 [2, 512, 9216], P(None, 'head', 'patch')
- patch_grad: float32 [2, 512, 9216], P(None, 'head', 'patch')
- qkv_grad: float32 [1536, 512], P('head')
- out_grad: float32 [512, 512], P('head')
- norm_grad: float32 [2, 512], replicated
- bias_grad: float32 [4, 512], P(None, 'head')
- kernel_grad: float32 [83, 512], P(None, 'head')
- conv_grad: float32 [8, 33], P('head')
- qkv_rows_new: float32 [1536], P('head')
- qkv_cols_new: float32 [512], replicated
- out_rows_new: float32 [512], P('head')
- out_cols_new: float32 [512], replicated
- norm_second_new: float32 [2, 512], replicated
- bias_second_new: float32 [4, 512], P(None, 'head')
- kernel_second_new: float32 [83, 512], P(None, 'head')
- conv_second_new: float32 [8, 33], P('head')
- qkv_new: float32 [1536, 512], P('head')
- out_new: float32 [512, 512], P('head')
- norm_new: float32 [2, 512], replicated
- bias_new: float32 [4, 512], P(None, 'head')
- kernel_new: float32 [83, 512], P(None, 'head')
- conv_new: float32 [8, 33], P('head')
Inputs may be any that keep to these rules, and one draw needn't show every extreme that they name: `seg_start`: in each slide strictly rising; the first is 0. `hole_mask`: the first token of every landmark segment of a slide is tissue. `norm_params`: gains are positive.
All inputs are finite; a program needn't handle non-finite values.
Results may differ from a plain program's by a relative error of at most 0.01065.
The roundings to bfloat16 on the way count: a program that leaves them out, or rounds other values in their place, can miss the bound.
Values may be sent and summed in bfloat16 or wider, within the bound.
No kernel may reach another device: no remote copies, remote signals or barrier semaphores. Data moves between devices by JAX's collectives and lax.ppermute only.
A program may use at most 320 MiB of HBM per device.

v0:
```python
import math

import jax
import jax.numpy as jnp
from jax import lax
from jax.sharding import PartitionSpec as P

HEADS = 8
HD = 64
PINV_ITERS = 6
STEP = 10


EPS_NORM = 1e-05
EPS_FACTOR = 1e-30
RATE = 0.5
HIGHEST = lax.Precision.HIGHEST
BLOCKS = ((0, 49), (49, 74), (74, 83))


def with_halo(cells, sides, width):
    for axis, dim in sides:
        count = lax.axis_size(axis)
        ends = count - 1
        head = lax.slice_in_dim(cells, 0, width, axis=dim)
        tail = lax.slice_in_dim(cells, cells.shape[dim] - width, cells.shape[dim], axis=dim)
        cells = jnp.concatenate(
            [
                lax.ppermute(tail, axis, [(i, (i + 1) % count) for i in range(ends)]),
                cells,
                lax.ppermute(head, axis, [((i + 1) % count, i) for i in range(ends)]),
            ],
            axis=dim,
        )
    return cells


def matmul(left_side, right_side):
    return jnp.matmul(left_side, right_side, precision=HIGHEST)


def pseudo_inverse_of(kernel_two):
    frobenius = jnp.sum(kernel_two * kernel_two, axis=(-2, -1), keepdims=True)
    approx = jnp.swapaxes(kernel_two, -1, -2) / frobenius
    identity = jnp.eye(kernel_two.shape[-1], dtype=kernel_two.dtype)
    for turn_index in range(PINV_ITERS):
        product = matmul(kernel_two, approx)
        inner_term = 7.0 * identity - product
        inner_term = 15.0 * identity - matmul(product, inner_term)
        inner_term = 13.0 * identity - matmul(product, inner_term)
        approx = 0.25 * matmul(approx, inner_term)
    return approx


def inverse_of_scores(landmark_scores):
    return pseudo_inverse_of(jax.nn.softmax(landmark_scores, axis=-1))


def full_kernel(kernels):
    channels = kernels.shape[1]
    large_part = kernels[0:49].reshape(7, 7, channels)
    middle_part = jnp.pad(kernels[49:74].reshape(5, 5, channels), ((1, 1), (1, 1), (0, 0)))
    small_part = jnp.pad(kernels[74:83].reshape(3, 3, channels), ((2, 2), (2, 2), (0, 0)))
    return large_part + middle_part + small_part


def line_conv(padded, tap_weights, row_count):
    running = jnp.zeros((padded.shape[0], row_count, padded.shape[2]), jnp.float32)
    for tap_index in range(33):
        running = (
            running
            + padded[:, tap_index : tap_index + row_count].astype(jnp.float32)
            * tap_weights[tap_index]
        )
    return running


def grid_conv(padded, kernel, grid_rows, grid_cols):
    running = jnp.zeros(padded.shape[:-2] + (grid_rows, grid_cols), jnp.float32)
    for row_shift in range(7):
        for col_shift in range(7):
            running = (
                running
                + kernel[row_shift, col_shift][:, None, None]
                * padded[..., row_shift : row_shift + grid_rows, col_shift : col_shift + grid_cols]
            )
    return running


def shrink(update, usq_sum, weight_sq, entries):
    clip_factor = jnp.maximum(1.0, jnp.sqrt(usq_sum / entries))
    return RATE * jnp.sqrt(weight_sq / entries) * update / clip_factor


def local(
    patches,
    hole_mask,
    seg_start,
    cotangent,
    qkv_weight,
    out_weight,
    norm_params,
    biases,
    kernels,
    conv_weight,
    qkv_rows,
    qkv_cols,
    out_rows,
    out_cols,
    norm_second,
    bias_second,
    kernel_second,
    conv_second,
):
    patch_count = lax.axis_size("patch")
    head_count = lax.axis_size("head")
    patch_index = lax.axis_index("patch")
    head_index = lax.axis_index("head")
    slide_count, feat_width, tokens_dev = patches.shape
    head_local = feat_width // HD
    grid_rows = math.isqrt(tokens_dev // patch_count)
    grid_cols = grid_rows * patch_count
    full_width = feat_width * head_count
    total_tokens = tokens_dev * patch_count
    offset = head_index * feat_width
    decay_rate = 1.0 - STEP ** (-0.8)
    mask_float = hole_mask.astype(jnp.float32)
    gate_mask = mask_float[:, :, None, None]
    head_scale = HD ** (-0.5)
    gathered = lax.all_gather(patches, "head", axis=1, tiled=True)
    gathered = jnp.swapaxes(gathered, 1, 2).astype(jnp.float32)
    mean_value = jnp.mean(gathered, axis=-1, keepdims=True)
    variance = jnp.mean(gathered * gathered, axis=-1, keepdims=True) - mean_value * mean_value
    inv_std = lax.rsqrt(variance + EPS_NORM)
    centered = (gathered - mean_value) * inv_std
    normed = (centered * norm_params[0] + norm_params[1]).astype(jnp.bfloat16)
    qkv_low = qkv_weight.astype(jnp.bfloat16)
    projected = jnp.einsum("snd,fd->snf", normed, qkv_low, preferred_element_type=jnp.float32)
    projected = projected.reshape(slide_count, tokens_dev, head_local, 3, HD)
    queries = (projected[:, :, :, 0] * gate_mask * head_scale).astype(jnp.bfloat16)
    key_rows = (projected[:, :, :, 1] * gate_mask).astype(jnp.bfloat16)
    value_rows = (projected[:, :, :, 2] * gate_mask).astype(jnp.bfloat16)
    position = patch_index * tokens_dev + jnp.arange(tokens_dev, dtype=jnp.int32)
    seg_end = jnp.concatenate(
        [seg_start[:, 1:], jnp.full((slide_count, 1), total_tokens, jnp.int32)], axis=1
    )
    member = (position[None, :, None] >= seg_start[:, None, :]) & (
        position[None, :, None] < seg_end[:, None, :]
    )
    onehot = member.astype(jnp.bfloat16)
    query_sum = jnp.einsum("snm,snhe->smhe", onehot, queries, preferred_element_type=jnp.float32)
    key_sum = jnp.einsum("snm,snhe->smhe", onehot, key_rows, preferred_element_type=jnp.float32)
    counts = jnp.einsum(
        "sn,snm->sm", hole_mask.astype(jnp.bfloat16), onehot, preferred_element_type=jnp.float32
    )
    query_sum, key_sum, counts = lax.psum((query_sum, key_sum, counts), "patch")
    query_marks = (query_sum / counts[:, :, None, None]).astype(jnp.bfloat16)
    key_marks = (key_sum / counts[:, :, None, None]).astype(jnp.bfloat16)
    value_flat = value_rows.reshape(slide_count, tokens_dev, feat_width)
    value_padded = with_halo(value_flat, (("patch", 1),), 16)
    tap_weights = jnp.repeat(jnp.transpose(conv_weight), HD, axis=1)
    residual = line_conv(value_padded, tap_weights, tokens_dev)
    scores_three = jnp.einsum(
        "smhe,snhe->shmn", query_marks, key_rows, preferred_element_type=jnp.float32
    )
    raised = jnp.exp(scores_three) * mask_float[:, None, None, :]
    weights_three = raised.astype(jnp.bfloat16)
    weight_sum = jnp.sum(weights_three.astype(jnp.float32), axis=-1)
    gathered_sum = jnp.einsum(
        "shmn,snhe->shme", weights_three, value_rows, preferred_element_type=jnp.float32
    )
    weight_sum, gathered_sum = lax.psum((weight_sum, gathered_sum), "patch")
    mark_values = gathered_sum / weight_sum[..., None]
    landmark_scores = jnp.einsum(
        "smhe,skhe->shmk", query_marks, key_marks, preferred_element_type=jnp.float32
    )
    pseudo_inverse, inverse_pull = jax.vjp(inverse_of_scores, landmark_scores)
    mixed_marks = matmul(pseudo_inverse, mark_values).astype(jnp.bfloat16)
    scores_one = jnp.einsum(
        "snhe,smhe->shnm", queries, key_marks, preferred_element_type=jnp.float32
    )
    probs_one = jax.nn.softmax(scores_one, axis=-1)
    kernel_one = probs_one.astype(jnp.bfloat16)
    attended = jnp.einsum(
        "shnm,shme->snhe", kernel_one, mixed_marks, preferred_element_type=jnp.float32
    )
    heads_out = (attended.reshape(slide_count, tokens_dev, feat_width) + residual).astype(
        jnp.bfloat16
    )
    out_low = out_weight.astype(jnp.bfloat16)
    partial_out = jnp.einsum("fd,snf->sdn", out_low, heads_out, preferred_element_type=jnp.float32)
    branch = lax.psum_scatter(partial_out, "head", scatter_dimension=1, tiled=True)
    section_one = patches.astype(jnp.float32) + branch + biases[0][None, :, None]
    kernel = full_kernel(kernels)
    grid_one = section_one.reshape(slide_count, feat_width, grid_rows, grid_cols)
    grid_back = cotangent.astype(jnp.float32).reshape(slide_count, feat_width, grid_rows, grid_cols)
    framed = with_halo(jnp.stack([grid_one, grid_back]), (("patch", 3),), 3)
    framed = jnp.pad(framed, ((0, 0), (0, 0), (0, 0), (0, 0), (3, 3)))
    bias_total = (biases[1] + biases[2] + biases[3])[:, None, None]
    grid_out = grid_one + grid_conv(framed[0], kernel, grid_rows, grid_cols) + bias_total
    block_out = grid_out.reshape(slide_count, feat_width, tokens_dev).astype(jnp.bfloat16)
    back_one = grid_back + grid_conv(framed[1], kernel[::-1, ::-1], grid_rows, grid_cols)
    kernel_terms = []
    for row_shift in range(7):
        for col_shift in range(7):
            kernel_terms.append(
                jnp.sum(
                    grid_back
                    * framed[
                        0,
                        :,
                        :,
                        row_shift : row_shift + grid_rows,
                        col_shift : col_shift + grid_cols,
                    ],
                    axis=(0, 2, 3),
                )
            )
    kernel_full = jnp.stack(kernel_terms).reshape(7, 7, feat_width)
    kernel_grad = jnp.concatenate(
        [
            kernel_full.reshape(49, feat_width),
            kernel_full[1:6, 1:6].reshape(25, feat_width),
            kernel_full[2:5, 2:5].reshape(9, feat_width),
        ],
        axis=0,
    )
    grid_bias = jnp.sum(grid_back, axis=(0, 2, 3))
    back_flat = back_one.reshape(slide_count, feat_width, tokens_dev)
    bias_grad = jnp.stack([jnp.sum(back_flat, axis=(0, 2)), grid_bias, grid_bias, grid_bias])
    grad_low = back_flat.astype(jnp.bfloat16)
    piece_rows = lax.all_gather(grad_low, "head", axis=1, tiled=True)
    head_grad = jnp.einsum("scn,fc->snf", piece_rows, out_low, preferred_element_type=jnp.float32)
    weight_piece = jnp.einsum(
        "snf,scn->fc", heads_out, piece_rows, preferred_element_type=jnp.float32
    )
    head_grad, out_grad = (head_grad, weight_piece)
    head_low = head_grad.astype(jnp.bfloat16)
    grad_padded = with_halo(head_low, (("patch", 1),), 16)
    value_from_conv = line_conv(grad_padded, tap_weights[::-1], tokens_dev)
    head_float = head_low.astype(jnp.float32)
    conv_terms = jnp.stack(
        [
            jnp.sum(
                head_float
                * value_padded[:, tap_index : tap_index + tokens_dev].astype(jnp.float32),
                axis=(0, 1),
            )
            for tap_index in range(33)
        ]
    )
    conv_grad = jnp.transpose(jnp.sum(conv_terms.reshape(33, head_local, HD), axis=-1))
    head_three = head_low.reshape(slide_count, tokens_dev, head_local, HD)
    grad_mixed = jnp.einsum(
        "shnm,snhe->shme", kernel_one, head_three, preferred_element_type=jnp.float32
    )
    grad_kernel_one = jnp.einsum(
        "snhe,shme->shnm", head_three, mixed_marks, preferred_element_type=jnp.float32
    )
    grad_scores_one = (
        probs_one * (grad_kernel_one - jnp.sum(probs_one * grad_kernel_one, axis=-1, keepdims=True))
    ).astype(jnp.bfloat16)
    grad_queries = jnp.einsum(
        "shnm,smhe->snhe", grad_scores_one, key_marks, preferred_element_type=jnp.float32
    )
    grad_key_marks = jnp.einsum(
        "shnm,snhe->smhe", grad_scores_one, queries, preferred_element_type=jnp.float32
    )
    grad_mixed, grad_key_marks = lax.psum((grad_mixed, grad_key_marks), "patch")
    grad_inverse = matmul(grad_mixed, jnp.swapaxes(mark_values, -1, -2))
    grad_values = matmul(jnp.swapaxes(pseudo_inverse, -1, -2), grad_mixed)
    (grad_landmark,) = inverse_pull(grad_inverse)
    grad_query_inv = jnp.einsum(
        "shmk,skhe->smhe", grad_landmark, key_marks.astype(jnp.float32), precision=HIGHEST
    )
    grad_key_inv = jnp.einsum(
        "shmk,smhe->skhe", grad_landmark, query_marks.astype(jnp.float32), precision=HIGHEST
    )
    grad_gathered = (grad_values / weight_sum[..., None]).astype(jnp.bfloat16)
    grad_weight_sum = -jnp.sum(grad_values * mark_values, axis=-1) / weight_sum
    grad_raised = (
        jnp.einsum("snhe,shme->shmn", value_rows, grad_gathered, preferred_element_type=jnp.float32)
        + grad_weight_sum[..., None]
    )
    grad_scores_three = (grad_raised * raised).astype(jnp.bfloat16)
    grad_values_three = jnp.einsum(
        "shmn,shme->snhe", weights_three, grad_gathered, preferred_element_type=jnp.float32
    )
    grad_keys = jnp.einsum(
        "shmn,smhe->snhe", grad_scores_three, query_marks, preferred_element_type=jnp.float32
    )
    grad_query_part = jnp.einsum(
        "shmn,snhe->smhe", grad_scores_three, key_rows, preferred_element_type=jnp.float32
    )
    grad_query_part = lax.psum(grad_query_part, "patch")
    grad_query_sum = ((grad_query_part + grad_query_inv) / counts[:, :, None, None]).astype(
        jnp.bfloat16
    )
    grad_key_sum = ((grad_key_marks + grad_key_inv) / counts[:, :, None, None]).astype(jnp.bfloat16)
    grad_queries = grad_queries + jnp.einsum(
        "snm,smhe->snhe", onehot, grad_query_sum, preferred_element_type=jnp.float32
    )
    grad_keys = grad_keys + jnp.einsum(
        "snm,smhe->snhe", onehot, grad_key_sum, preferred_element_type=jnp.float32
    )
    grad_values_all = grad_values_three + value_from_conv.reshape(
        slide_count, tokens_dev, head_local, HD
    )
    grad_projected = jnp.stack(
        [
            grad_queries.astype(jnp.bfloat16).astype(jnp.float32) * gate_mask * head_scale,
            grad_keys.astype(jnp.bfloat16).astype(jnp.float32) * gate_mask,
            grad_values_all.astype(jnp.bfloat16).astype(jnp.float32) * gate_mask,
        ],
        axis=3,
    )
    grad_projected = grad_projected.reshape(slide_count, tokens_dev, 3 * feat_width).astype(
        jnp.bfloat16
    )
    qkv_grad = jnp.einsum("snf,snd->fd", grad_projected, normed, preferred_element_type=jnp.float32)
    grad_normed = jnp.einsum(
        "snf,fd->snd", grad_projected, qkv_low, preferred_element_type=jnp.float32
    )
    centered_own = lax.dynamic_slice_in_dim(centered, offset, feat_width, 2)
    gain_own = lax.dynamic_slice_in_dim(norm_params[0], offset, feat_width, 0)
    weighted = grad_normed * norm_params[0]
    moments = jnp.stack(
        [jnp.sum(weighted, axis=-1), jnp.sum(weighted * centered, axis=-1)], axis=-1
    )
    own_grad, moments = (
        lax.psum_scatter(grad_normed, "head", scatter_dimension=2, tiled=True),
        lax.psum_scatter(
            jnp.tile(moments, (1, 1, head_count)), "head", scatter_dimension=2, tiled=True
        ),
    )
    own_term = inv_std * (
        own_grad * gain_own
        - moments[..., 0:1] / full_width
        - centered_own * moments[..., 1:2] / full_width
    )
    patch_grad = jnp.swapaxes(own_term, 1, 2) + back_flat
    norm_own = jnp.stack(
        [jnp.sum(own_grad * centered_own, axis=(0, 1)), jnp.sum(own_grad, axis=(0, 1))]
    )
    norm_grad = lax.dynamic_update_slice_in_dim(
        jnp.zeros((2, full_width), jnp.float32), norm_own, offset, 1
    )
    qkv_grad, out_grad, norm_grad, bias_grad, kernel_grad, conv_grad = lax.psum(
        (qkv_grad, out_grad, norm_grad, bias_grad, kernel_grad, conv_grad), "patch"
    )
    qkv_squares = qkv_grad * qkv_grad
    qkv_rows_new = decay_rate * qkv_rows + (1.0 - decay_rate) * (
        jnp.mean(qkv_squares, axis=1) + EPS_FACTOR
    )
    out_squares = out_grad * out_grad
    out_rows_new = decay_rate * out_rows + (1.0 - decay_rate) * (
        jnp.mean(out_squares, axis=1) + EPS_FACTOR
    )
    bias_second_new = decay_rate * bias_second + (1.0 - decay_rate) * (
        bias_grad * bias_grad + EPS_FACTOR
    )
    bias_update = bias_grad * lax.rsqrt(bias_second_new)
    kernel_second_new = decay_rate * kernel_second + (1.0 - decay_rate) * (
        kernel_grad * kernel_grad + EPS_FACTOR
    )
    kernel_update = kernel_grad * lax.rsqrt(kernel_second_new)
    conv_second_new = decay_rate * conv_second + (1.0 - decay_rate) * (
        conv_grad * conv_grad + EPS_FACTOR
    )
    conv_update = conv_grad * lax.rsqrt(conv_second_new)
    kernel_usq = jnp.stack(
        [
            jnp.sum(kernel_update[start_row:end_row] * kernel_update[start_row:end_row])
            for start_row, end_row in BLOCKS
        ]
    )
    kernel_wsq = jnp.stack(
        [
            jnp.sum(kernels[start_row:end_row] * kernels[start_row:end_row])
            for start_row, end_row in BLOCKS
        ]
    )
    (
        qkv_colsum,
        qkv_part,
        qkv_rowtotal,
        qkv_wsq,
        out_colsum,
        out_part,
        out_rowtotal,
        out_wsq,
        bias_usq,
        bias_wsq,
        kernel_usq,
        kernel_wsq,
        conv_usq,
        conv_wsq,
        norm_grad,
    ) = lax.psum(
        (
            jnp.sum(qkv_squares, axis=0),
            jnp.sum(qkv_squares / qkv_rows_new[:, None], axis=0),
            jnp.sum(qkv_rows_new),
            jnp.sum(qkv_weight * qkv_weight),
            jnp.sum(out_squares, axis=0),
            jnp.sum(out_squares / out_rows_new[:, None], axis=0),
            jnp.sum(out_rows_new),
            jnp.sum(out_weight * out_weight),
            jnp.sum(bias_update * bias_update, axis=1),
            jnp.sum(biases * biases, axis=1),
            kernel_usq,
            kernel_wsq,
            jnp.sum(conv_update * conv_update),
            jnp.sum(conv_weight * conv_weight),
            norm_grad,
        ),
        "head",
    )
    qkv_mean = qkv_rowtotal / (3 * full_width)
    qkv_cols_new = decay_rate * qkv_cols + (1.0 - decay_rate) * (
        qkv_colsum / (3 * full_width) + EPS_FACTOR
    )
    qkv_usq = qkv_mean * jnp.sum(qkv_part / qkv_cols_new)
    qkv_update = qkv_grad * lax.rsqrt(qkv_rows_new[:, None] * qkv_cols_new[None, :] / qkv_mean)
    qkv_new = qkv_weight - shrink(qkv_update, qkv_usq, qkv_wsq, 3 * full_width * full_width)
    out_mean = out_rowtotal / full_width
    out_cols_new = decay_rate * out_cols + (1.0 - decay_rate) * (
        out_colsum / full_width + EPS_FACTOR
    )
    out_usq = out_mean * jnp.sum(out_part / out_cols_new)
    out_update = out_grad * lax.rsqrt(out_rows_new[:, None] * out_cols_new[None, :] / out_mean)
    out_new = out_weight - shrink(out_update, out_usq, out_wsq, full_width * full_width)
    norm_second_new = decay_rate * norm_second + (1.0 - decay_rate) * (
        norm_grad * norm_grad + EPS_FACTOR
    )
    norm_update = norm_grad * lax.rsqrt(norm_second_new)
    norm_new = norm_params - shrink(
        norm_update,
        jnp.sum(norm_update * norm_update, axis=1, keepdims=True),
        jnp.sum(norm_params * norm_params, axis=1, keepdims=True),
        full_width,
    )
    bias_new = biases - shrink(bias_update, bias_usq[:, None], bias_wsq[:, None], full_width)
    kernel_pieces = []
    for block_index in range(3):
        start_row, end_row = BLOCKS[block_index]
        kernel_pieces.append(
            kernels[start_row:end_row]
            - shrink(
                kernel_update[start_row:end_row],
                kernel_usq[block_index],
                kernel_wsq[block_index],
                (end_row - start_row) * full_width,
            )
        )
    kernel_new = jnp.concatenate(kernel_pieces, axis=0)
    conv_new = conv_weight - shrink(conv_update, conv_usq, conv_wsq, HEADS * 33)
    return (
        block_out,
        patch_grad,
        qkv_grad,
        out_grad,
        norm_grad,
        bias_grad,
        kernel_grad,
        conv_grad,
        qkv_rows_new,
        qkv_cols_new,
        out_rows_new,
        out_cols_new,
        norm_second_new,
        bias_second_new,
        kernel_second_new,
        conv_second_new,
        qkv_new,
        out_new,
        norm_new,
        bias_new,
        kernel_new,
        conv_new,
    )


def solution(mesh):
    placed = (
        P(None, "head", "patch"),
        P(None, "patch"),
        P(),
        P(None, "head", "patch"),
        P("head", None),
        P("head", None),
        P(),
        P(None, "head"),
        P(None, "head"),
        P("head", None),
        P("head"),
        P(),
        P("head"),
        P(),
        P(),
        P(None, "head"),
        P(None, "head"),
        P("head", None),
    )
    return jax.shard_map(
        local,
        mesh=mesh,
        in_specs=placed,
        out_specs=(
            P(None, "head", "patch"),
            P(None, "head", "patch"),
            P("head", None),
            P("head", None),
            P(),
            P(None, "head"),
            P(None, "head"),
            P("head", None),
            P("head"),
            P(),
            P("head"),
            P(),
            P(),
            P(None, "head"),
            P(None, "head"),
            P("head", None),
            P("head", None),
            P("head", None),
            P(),
            P(None, "head"),
            P(None, "head"),
            P("head", None),
        ),
        check_vma=False,
    )
```

profile of v0, /device:TPU:0, one launch (start us, length us, event | category | flops | bytes accessed | tf_op | source)
XLA Modules:
  0.0 968.6 jit_solution(9563617127974595212)
XLA Ops:
  33.8 15.5 %psum.204 = f32[2,256]{1,0:T(2,128)S(1)} all-reduce(f32[2,256]{1,0:T(2,128)S(1)} %bitcast.645), channel_id=1, replica_groups=mesh['patch'=8,'head'=4] {'patch'}, use_global_device_ids=true, to_apply=%region_3.0 | all-reduce | flops 512 | bytes 4096 | tf_op jit(solution)/shard_map/psum | solution.py:156
  49.5 14.0 %all-gather.3.cloned.1.call-done = bf16[2,512,1152]{1,2,0:T(8,128)(2,1)} async-done(((bf16[2,128,1152]{1,2,0:T(8,128)(2,1)}), bf16[2,512,1152]{1,2,0:T(8,128)(2,1)}) %all-gather.3.cloned.1.call-update) | async-done | bytes 2359312 | tf_op jit(solution)/shard_map/all_gather | solution.py:130
  75.6 50.4 %all-reduce.17.cloned.1.call-done = f32[2,256,2,64]{1,3,2,0:T(8,128)} async-done(((f32[2,256,2,64]{1,3,2,0:T(8,128)}), f32[2,256,2,64]{1,3,2,0:T(8,128)}) %all-reduce.17.cloned.1.call-update) | async-done | bytes 262160 | tf_op jit(solution)/shard_map/psum | solution.py:156
  137.9 13.9 %psum.207 = f32[2,2,256]{2,1,0:T(2,128)S(1)} all-reduce(f32[2,2,256]{2,1,0:T(2,128)S(1)} %get-tuple-element.413), channel_id=1, replica_groups=mesh['patch'=8,'head'=4] {'patch'}, use_global_device_ids=true, to_apply=%region_10.0 | all-reduce | flops 1024 | bytes 8192 | tf_op jit(solution)/shard_map/psum | solution.py:172
  151.9 34.0 %all-reduce.27.cloned.1.call-done = (f32[2,256,2,64]{1,3,2,0:T(8,128)}, f32[2,2,256,64]{2,3,1,0:T(8,128)}) async-done(((f32[2,256,2,64]{1,3,2,0:T(8,128)}, f32[2,2,256,64]{2,3,1,0:T(8,128)}), (f32[2,256,2,64]{1,3,2,0:T(8,128)}, f32[2,2,256,64]{2,3,1,0:T(8,128)})) %all-reduce.27.cloned.1.call-update) | async-done | bytes 524304 | tf_op jit(solution)/shard_map/psum | solution.py:156
  207.6 4.7 online-softmax.1
  219.4 4.8 online-softmax.2
  255.4 5.0 online-softmax.5
  275.5 23.1 %fusion.135 = bf16[2,1152,128]{2,1,0:T(8,128)(2,1)S(1)} fusion(f32[2,1152,128]{2,1,0:T(8,128)} %copy.200, bf16[2,1152,128]{2,1,0:T(8,128)(2,1)} %copy-done.18, bf16[2,16,128]{2,1,0:T(8,128)(2,1)S(1)} %collective-permute-done.1, bf16[2,16,128]{2,1,0:T(8,128)(2,1)} %collective-permute-done, f32[128]{0:T(128)} %broadcast_in_dim.260, f32[128]{0:T(128)} %broadcast_in_dim.258, ...), kind=kLoop, calls=%fused_computation.361 | loop fusion | flops 57802752 | bytes 2392576 | tf_op jit(solution)/shard_map/convert_element_type | solution.py:187
  328.1 59.1 %reduce-scatter.3.cloned.1.call-done = f32[2,128,1152]{1,2,0:T(8,128)} async-done(((f32[2,512,1152]{1,2,0:T(8,128)}), f32[2,128,1152]{1,2,0:T(8,128)}) %reduce-scatter.3.cloned.1.call-update) | async-done | bytes 1179664 | tf_op jit(solution)/shard_map/reduce_scatter | solution.py:192
  402.8 9.2 fusion.466
  424.3 7.7 fusion.468
  432.0 7.7 fusion.469
  439.9 8.4 fusion.233
  454.9 20.3 %all-gather.5.cloned.1.call-done = bf16[2,512,1152]{1,2,0:T(8,128)(2,1)} async-done(((bf16[2,128,1152]{1,2,0:T(8,128)(2,1)}), bf16[2,512,1152]{1,2,0:T(8,128)(2,1)}) %all-gather.5.cloned.1.call-update) | async-done | bytes 2359312 | tf_op jit(solution)/shard_map/all_gather | solution.py:232
  499.6 12.0 %fusion.152 = f32[2,1152,128]{2,1,0:T(8,128)} fusion(bf16[2,1152,128]{2,1,0:T(8,128)(2,1)S(1)} %copy-done.21, bf16[2,16,128]{2,1,0:T(8,128)(2,1)} %collective-permute-done.5, bf16[2,16,128]{2,1,0:T(8,128)(2,1)} %collective-permute-done.4, f32[128]{0:T(128)S(1)} %copy-done.295, f32[128]{0:T(128)S(1)} %copy-done.296, f32[128]{0:T(128)S(1)} %copy-done.297, ...), kind=kLoop, calls=%fused_computation.378 | loop fusion | flops 57212928 | bytes 1802752 | tf_op jit(solution)/shard_map/add | solution.py:71
  514.3 29.8 %all-reduce.19.cloned.1.call-done = f32[2,2,256,64]{2,3,1,0:T(8,128)} async-done(((f32[2,2,256,64]{2,3,1,0:T(8,128)}), f32[2,2,256,64]{2,3,1,0:T(8,128)}) %all-reduce.19.cloned.1.call-update) | async-done | bytes 262160 | tf_op jit(solution)/shard_map/psum | solution.py:269
  637.3 50.8 %all-reduce.25.cloned.1.call-done = (f32[2,256,2,64]{1,3,2,0:T(8,128)}, f32[2,256,2,64]{1,3,2,0:T(8,128)}) async-done(((f32[2,256,2,64]{1,3,2,0:T(8,128)}, f32[2,256,2,64]{1,3,2,0:T(8,128)}), (f32[2,256,2,64]{1,3,2,0:T(8,128)}, f32[2,256,2,64]{1,3,2,0:T(8,128)})) %all-reduce.25.cloned.1.call-update) | async-done | bytes 524304 | tf_op jit(solution)/shard_map/psum | solution.py:269
  708.2 6.7 fusion.232
  717.7 9.4 fusion.287
  742.3 55.4 %all-reduce.23.cloned.1.call-done = (f32[384,512]{1,0:T(8,128)}, f32[128,512]{1,0:T(8,128)}) async-done(((f32[384,512]{1,0:T(8,128)}, f32[128,512]{1,0:T(8,128)}), (f32[384,512]{1,0:T(8,128)}, f32[128,512]{1,0:T(8,128)})) %all-reduce.23.cloned.1.call-update) | async-done | bytes 1048592 | tf_op jit(solution)/shard_map/psum | solution.py:348
  802.7 81.6 %reduce-scatter.5.cloned.1.call-done = f32[2,1152,128]{2,1,0:T(8,128)} async-done(((f32[2,1152,512]{2,1,0:T(8,128)}), f32[2,1152,128]{2,1,0:T(8,128)}) %reduce-scatter.5.cloned.1.call-update) | async-done | bytes 1179664 | tf_op jit(solution)/shard_map/reduce_scatter | solution.py:331
  886.4 25.1 %all-reduce.5 = (f32[2,512]{1,0:T(2,128)}, f32[4,128]{1,0:T(4,128)}, f32[83,128]{1,0:T(8,128)}, f32[2,33]{1,0:T(2,128)}) all-reduce(f32[2,512]{1,0:T(2,128)S(1)} %maximum_dynamic-update-slice_fusion, f32[4,128]{1,0:T(4,128)} %pad_maximum_fusion.10, f32[83,128]{1,0:T(8,128)S(1)} %concatenate.106, ...), channel_id=1, replica_groups=mesh['patch'=8,'head'=4] {'patch'}, use_global_device_ids=true, to_apply=%region_29.30 | all-reduce | flops 12226 | bytes 97808 | tf_op jit(solution)/shard_map/psum | solution.py:348
  923.5 19.6 %all-reduce.9 = (f32[2,512]{1,0:T(2,128)S(1)}, f32[512]{0:T(512)S(1)}, f32[512]{0:T(512)S(1)}, f32[]{:T(128)}, f32[512]{0:T(512)S(1)}, /*index=5*/f32[]{:T(128)}...) all-reduce(f32[2,512]{1,0:T(2,128)S(1)} %copy-done.263, ...), channel_id=1, replica_groups=mesh['patch'=8,'head'=4] {'head'}, use_global_device_ids=true, to_apply=%region_30.31 | all-reduce | flops 3092 | bytes 24736 | tf_op jit(solution)/shard_map/psum | solution.py:399
  (1043 shorter events, 371.2 us)
Async XLA Ops:
  7.2 56.3 %all-gather.3.cloned.1.call-start = ((), (), s32[]{:S(2)}) async-start(), calls=%async_computation.2 | async-start | bytes 2949120 | tf_op jit(solution)/shard_map/all_gather | solution.py:130
  9.4 116.6 %all-reduce.17.cloned.1.call-start = ((), (), s32[]{:S(2)}) async-start(), calls=%async_computation.3 | async-start | bytes 524288 | tf_op jit(solution)/shard_map/psum | solution.py:156
  33.1 98.6 %copy-start.130 = (f32[2,1152]{1,0:T(2,128)}, f32[2,1152]{1,0:T(2,128)S(1)}, u32[]{:S(2)}) copy-start(f32[2,1152]{1,0:T(2,128)S(1)} %get-tuple-element.398) | copy-start | bytes 27652
  49.4 136.5 %copy-start.152 = (f32[2,256]{1,0:T(2,128)}, f32[2,256]{1,0:T(2,128)S(1)}, u32[]{:S(2)}) copy-start(f32[2,256]{1,0:T(2,128)S(1)} %psum.204) | copy-start | bytes 6148
  49.4 177.8 %copy-start.41 = (f32[256,256]{1,0:T(8,128)}, f32[256,256]{1,0:T(8,128)S(1)}, u32[]{:S(2)}) copy-start(f32[256,256]{1,0:T(8,128)S(1)} %fusion.432) | copy-start | bytes 786436
  49.5 186.7 %copy-start.40 = (f32[256,256]{1,0:T(8,128)}, f32[256,256]{1,0:T(8,128)S(1)}, u32[]{:S(2)}) copy-start(f32[256,256]{1,0:T(8,128)S(1)} %fusion.431) | copy-start | bytes 786436
  72.6 116.1 %copy-start.83 = (bf16[2,1152,2,64]{1,3,2,0:T(8,128)(2,1)}, bf16[2,1152,2,64]{1,3,2,0:T(8,128)(2,1)S(1)}, u32[]{:S(2)}) copy-start(bf16[2,1152,2,64]{1,3,2,0:T(8,128)(2,1)S(1)} %get-tuple-element.324) | copy-start | bytes 1769476
  74.1 111.8 %all-reduce.27.cloned.1.call-start = ((), (), s32[]{:S(2)}) async-start(), calls=%async_computation.11 | async-start | bytes 1048576 | tf_op jit(solution)/shard_map/psum | solution.py:156
  131.7 255.5 %reduce-scatter.3.cloned.1.call-start = ((), (), s32[]{:S(2)}) async-start(), calls=%async_computation.4 | async-start | bytes 5898240 | tf_op jit(solution)/shard_map/reduce_scatter | solution.py:192
  134.8 140.7 %collective-permute-start = (bf16[2,16,128]{2,1,0:T(8,128)(2,1)}, bf16[2,16,128]{2,1,0:T(8,128)(2,1)}, u32[]{:S(2)}, u32[]{:S(2)}) collective-permute-start(bf16[2,16,128]{2,1,0:T(8,128)(2,1)} %get-tuple-element.338), channel_id=1, source_target_pairs={{0,4},{4,8},{8,12},{12,16},{16,20},{20,24},{24,28},{1,5},{5,9},{9,... | collective-permute-start | bytes 24584 | tf_op jit(solution)/shard_map/ppermute | solution.py:29
  136.7 138.9 %collective-permute-start.1 = (bf16[2,16,128]{2,1,0:T(8,128)(2,1)}, bf16[2,16,128]{2,1,0:T(8,128)(2,1)S(1)}, u32[]{:S(2)}, u32[]{:S(2)}) collective-permute-start(bf16[2,16,128]{2,1,0:T(8,128)(2,1)} %get-tuple-element.339), channel_id=1, source_target_pairs={{4,0},{8,4},{12,8},{16,12},{20,16},{24,20},{28,24},{5,1},{9,5},{13... | collective-permute-start | bytes 24584 | tf_op jit(solution)/shard_map/ppermute | solution.py:31
  302.5 172.8 %all-gather.5.cloned.1.call-start = ((), (), s32[]{:S(2)}) async-start(), calls=%async_computation.5 | async-start | bytes 2949120 | tf_op jit(solution)/shard_map/all_gather | solution.py:232
  326.8 75.6 %copy-start.220 = (f32[128]{0:T(128)}, f32[128]{0:T(128)S(1)}, u32[]{:S(2)}) copy-start(f32[128]{0:T(128)S(1)} %get-tuple-element.386) | copy-start | bytes 1540
  390.2 7.1 collective-permute-start.2
  392.8 4.6 collective-permute-start.3
  414.0 130.1 %all-reduce.19.cloned.1.call-start = ((), (), s32[]{:S(2)}) async-start(), calls=%async_computation.6 | async-start | bytes 524288 | tf_op jit(solution)/shard_map/psum | solution.py:269
  482.8 16.4 %collective-permute-start.4 = (bf16[2,16,128]{2,1,0:T(8,128)(2,1)}, bf16[2,16,128]{2,1,0:T(8,128)(2,1)}, u32[]{:S(2)}, u32[]{:S(2)}) collective-permute-start(bf16[2,16,128]{2,1,0:T(8,128)(2,1)} %get-tuple-element.336), channel_id=1, source_target_pairs={{0,4},{4,8},{8,12},{12,16},{16,20},{20,24},{24,28},{1,5},{5,9},{9,... | collective-permute-start | bytes 24584 | tf_op jit(solution)/shard_map/ppermute | solution.py:29
  484.8 14.5 %collective-permute-start.5 = (bf16[2,16,128]{2,1,0:T(8,128)(2,1)}, bf16[2,16,128]{2,1,0:T(8,128)(2,1)}, u32[]{:S(2)}, u32[]{:S(2)}) collective-permute-start(bf16[2,16,128]{2,1,0:T(8,128)(2,1)} %get-tuple-element.337), channel_id=1, source_target_pairs={{4,0},{8,4},{12,8},{16,12},{20,16},{24,20},{28,24},{5,1},{9,5},{13... | collective-permute-start | bytes 24584 | tf_op jit(solution)/shard_map/ppermute | solution.py:31
  489.8 198.2 %all-reduce.25.cloned.1.call-start = ((), (), s32[]{:S(2)}) async-start(), calls=%async_computation.10 | async-start | bytes 1048576 | tf_op jit(solution)/shard_map/psum | solution.py:269
  633.9 107.7 %all-reduce.21.cloned.1.call-start = ((), (), s32[]{:S(2)}) async-start(), calls=%async_computation.8 | async-start | bytes 147456
  703.4 94.3 %all-reduce.23.cloned.1.call-start = ((), (), s32[]{:S(2)}) async-start(), calls=%async_computation.9 | async-start | bytes 2097152 | tf_op jit(solution)/shard_map/psum | solution.py:348
  707.2 177.1 %reduce-scatter.5.cloned.1.call-start = ((), (), s32[]{:S(2)}) async-start(), calls=%async_computation.7 | async-start | bytes 5898240 | tf_op jit(solution)/shard_map/reduce_scatter | solution.py:331
  738.2 63.2 %copy-start.274 = (f32[384]{0:T(512)S(1)}, f32[384]{0:T(512)}, u32[]{:S(2)}) copy-start(f32[384]{0:T(512)} %param.28) | copy-start | bytes 4612
  801.9 156.9 %copy-start.154 = (f32[384]{0:T(512)}, f32[384]{0:T(512)S(1)}, u32[]{:S(2)}) copy-start(f32[384]{0:T(512)S(1)} %get-tuple-element.438) | copy-start | bytes 4612
  (319 other events, 1971.9 us)
Sparse Core Ops, SparseCore 0:
  10.2 53.2 all-gather.2
  74.2 51.7 all-reduce.16
  131.8 54.0 all-reduce.26
  302.6 84.5 reduce-scatter.2
  414.1 61.1 all-gather.4
  489.9 54.1 all-reduce.18
  634.0 54.0 all-reduce.24
  703.5 33.2 all-reduce.20
  740.9 56.7 all-reduce.22
  799.9 84.3 reduce-scatter.4
where the time goes:
time: 978 us; the launch traced here: 969 us
  waiting for transfers between devices  396 us (40%)
  matrix products  176 us (18%)
  other arithmetic  139 us (14%)
  local copies, waits for them, and re-layouts  115 us (12%)
  blocking collectives  74.2 us (8%)
  between operations  29.1 us (3%)
  Pallas kernels  28.4 us (3%)
  starting transfers between devices  11.3 us (1%)
    dot_general x69, matrix products, matmul(): return jnp.matmul(left_side, right_side, precision=HIGHEST)  119 us
    psum x2, waiting for transfers between devices, local(): query_sum, key_sum, counts = lax.psum((query_sum, key_sum, counts), 'patch')  84.4 us
    reduce_scatter x1, waiting for transfers between devices, local(): lax.psum_scatter(grad_normed, 'head', scatter_dimension=2, tiled=True)  81.6 us
    psum x2, waiting for transfers between devices, local(): grad_mixed, grad_key_marks = lax.psum((grad_mixed, grad_key_marks), 'patch')  80.6 us
    reduce_scatter x1, waiting for transfers between devices, local(): lax.psum_scatter(partial_out, 'head', scatter_dimension=1, tiled=True)  59.1 us
    psum x1, waiting for transfers between devices, local(): lax.psum((qkv_grad, out_grad, norm_grad, bias_grad, kernel_grad, conv_gra...  55.4 us
    unnamed x693, local copies, waits for them, and re-layouts  41.7 us
    unnamed x6, Pallas kernels  28.4 us
  transfers between devices with their start and end apart: 16, of which 10 were waited for; matrix products, arithmetic and copies ran while one was open for 22% of the time, Pallas kernels for 3%

commit v1 on v0

v1 whole, which is shorter than its diff:
```python
import functools
import math

import jax
import jax.numpy as jnp
from jax import lax
from jax.experimental import pallas as pl
from jax.experimental.pallas import tpu as pltpu
from jax.sharding import PartitionSpec as P

HEADS = 8
HD = 64
PINV_ITERS = 6
STEP = 10
TAPS = 33
REACH = 16

EPS_NORM = 1e-05
EPS_FACTOR = 1e-30
RATE = 0.5
BLOCKS = ((0, 49), (49, 74), (74, 83))

SMALL = 16
CONV_ROW = 13
NORM_ROW = 14
ROOM = 16
GRID_ROOM = 18
LARGE_ROOM = 56
PULL_ROOM = 56
MARK_ROOM = 56
PULL_MICROS = 2
F32 = jnp.float32
BF16 = jnp.bfloat16


def swap(value, axis, bit):
    return swap_bits(value, axis, 1 << bit)


def swap_bits(value, axis, bits):
    count = lax.axis_size(axis)
    return lax.ppermute(value, axis, [(i, i ^ bits) for i in range(count)])


def bit_of(axis, bit):
    return (lax.axis_index(axis) >> bit) & 1


def keep_half(value, axis, bit):
    mine = bit_of(axis, bit)
    kept = lax.dynamic_index_in_dim(value, mine, 0, keepdims=False)
    sent = lax.dynamic_index_in_dim(value, 1 - mine, 0, keepdims=False)
    return kept + swap(sent, axis, bit)


def join_half(value, axis, bit):
    other = swap(value, axis, bit)
    first = bit_of(axis, bit) == 0
    return jnp.stack([jnp.where(first, value, other), jnp.where(first, other, value)])


def all_sum(value, axis, first_bit=0):
    bits = (lax.axis_size(axis) - 1).bit_length()
    for bit in range(first_bit, bits):
        value = value + swap(value, axis, bit)
    return value


def sum_to_owner(scalars, kept, sent, after=None, direct=()):
    received = swap(sent, "patch", 0)
    count = lax.axis_size("patch")
    if kept.shape[0] != 2:
        return all_sum((kept + received)[0], "patch", 1)
    flat = (2 * kept.shape[1], kept.shape[2])
    kept, sent = fold_halves(
        scalars, kept.reshape(flat), received.reshape(flat), 1, scalars, F32
    )
    if direct and count >= 8:
        near, far = swap_bits(sent, "patch", 2), swap_bits(sent, "patch", 6)
        value = add_four(kept, swap_bits(kept, "patch", 4), near, far, direct)
        return all_sum(value, "patch", 3)
    received = swap(sent, "patch", 1)
    value = kept + received if after is None else add_parts(kept, received, after)
    return all_sum(value, "patch", 2)


def from_owner(value, heads, scalars, after):
    if heads == 2:
        value = join_heads(scalars, value, swap(value, "patch", 1), after)
    else:
        value = value[None]
    return join_half(value, "patch", 0)


def sum_rows(scalars, kept, sent, small, axis, orders):
    bits = (lax.axis_size(axis) - 1).bit_length()
    for bit in range(1, bits):
        received = swap(sent, axis, bit - 1)
        after = orders[bit - 1] if bit <= len(orders) else scalars
        kept, sent = fold_halves(scalars, kept, received, bit, after)
    value = (kept + swap(sent, axis, bits - 1).astype(F32)).astype(BF16)
    for bit in reversed(range(bits)):
        rows = value.shape[0]
        small = lax.reduce_precision(small, 8, 7)
        other = swap(jnp.concatenate([value, small.astype(BF16)], axis=0), axis, bit)
        small = small + other[rows:].astype(F32)
        other = other[:rows]
        first = bit_of(axis, bit) == 0
        value = jnp.concatenate(
            [jnp.where(first, value, other), jnp.where(first, other, value)], axis=0
        )
    return value, small


def neighbours(value, width, kind=BF16):
    count = lax.axis_size("patch")
    odd = bit_of("patch", 0) == 1
    last = value.shape[-1] - width
    axis = value.ndim - 1
    inner = lax.dynamic_slice_in_dim(value, jnp.where(odd, 0, last), width, axis)
    outer = lax.dynamic_slice_in_dim(value, jnp.where(odd, last, 0), width, axis)
    inner, outer = inner.astype(kind), outer.astype(kind)
    inner = swap(inner, "patch", 0)
    steps = [(i, i + 1) for i in range(1, count - 1, 2)]
    outer = lax.ppermute(outer, "patch", steps + [(j, i) for i, j in steps])
    return inner, outer


def in_order(scalars_ref, inner, outer):
    odd = scalars_ref[2] == 1
    return jnp.where(odd, inner, outer), jnp.where(odd, outer, inner)


NN = (((1,), (0,)), ((), ()))
NT = (((1,), (1,)), ((), ()))
TN = (((0,), (0,)), ((), ()))


def dot(left, right, dims=NN):
    return lax.dot_general(left, right, dims, preferred_element_type=F32)


def parts(value):
    high = value.astype(BF16)
    return high, (value - high.astype(F32)).astype(BF16)


def dot3(left, right, dims=NN):
    return dot(left[0], right[0], dims) + (
        dot(left[0], right[1], dims) + dot(left[1], right[0], dims)
    )


def eye(size):
    rows = lax.broadcasted_iota(jnp.int32, (size, size), 0)
    cols = lax.broadcasted_iota(jnp.int32, (size, size), 1)
    return (rows == cols).astype(F32)


HALF = PINV_ITERS // 2


def inverse_turns(product, inverse, turns, q_ref, p_ref):
    identity = eye(product.shape[0])
    for turn in range(turns):
        p_ref[turn] = product
        now = parts(product)
        square = dot3(now, now)
        square_parts = parts(square)
        cube = dot3(square_parts, now)
        fourth = dot3(square_parts, square_parts)
        factor = 0.25 * (13.0 * identity - 15.0 * product + 7.0 * square - cube)
        q_ref[turn] = factor
        inverse = dot3(parts(inverse), parts(factor))
        product = 0.25 * (13.0 * product - 15.0 * square + 7.0 * cube - fourth)
    return product, inverse


def inverse_early_kernel(marks_ref, kernel_ref, q_ref, p_ref, carried_ref, done_ref):
    done_ref[...] = jnp.zeros_like(done_ref)
    marks = marks_ref[...]
    scores = dot(marks[:HD], marks[HD:], TN)
    raised = jnp.exp(scores - jnp.max(scores, axis=-1, keepdims=True))
    kernel = raised * (1.0 / jnp.sum(raised, axis=-1, keepdims=True))
    kernel_ref[...] = kernel
    scale = 1.0 / norm_of(kernel)
    halves = parts(kernel)
    product = dot3(halves, halves, NT) * scale
    carried_ref[0], carried_ref[1] = inverse_turns(product, kernel.T * scale, HALF, q_ref, p_ref)


def inverse_late_kernel(carried_ref, z_ref, q_ref, p_ref):
    turns = PINV_ITERS - HALF
    _, z_ref[...] = inverse_turns(carried_ref[0], carried_ref[1], turns, q_ref, p_ref)


def norm_of(kernel):
    return jnp.sum(jnp.sum(kernel * kernel, axis=0, keepdims=True), axis=1, keepdims=True)


def mixed_marks_kernel(sums_ref, z_ref, out_ref):
    values = sums_ref[:HD] / sums_ref[HD : HD + 1]
    out_ref[...] = dot3(parts(values), parts(z_ref[...]), NT).astype(BF16)


def grad_values_kernel(sums_ref, grads_ref, z_ref, out_ref):
    weight_sum = sums_ref[HD : HD + 1]
    values = sums_ref[:HD] / weight_sum
    left = dot3(parts(grads_ref[...]), parts(z_ref[...]))
    high, low = parts(-jnp.sum(left * values, axis=0, keepdims=True) / weight_sum)
    rows = out_ref.shape[0] - HD
    row = lax.broadcasted_iota(jnp.int32, (rows, out_ref.shape[1]), 0)
    tail = jnp.where(row == 0, high.astype(F32), jnp.where(row == 1, low.astype(F32), 0.0))
    out_ref[:HD] = (left / weight_sum).astype(BF16)
    out_ref[HD:] = tail.astype(BF16)


def total_of(value):
    return jnp.sum(jnp.sum(value, axis=0, keepdims=True), axis=1, keepdims=True)


def even(value):
    return 0.5 * (value + value.T)


def pull_turns(carried, turns, q_ref, p_ref, thin_ref, first):
    for turn in reversed(range(turns)):
        product = parts(p_ref[turn])
        left, right = thin_ref[first + turn], thin_ref[PINV_ITERS + first + turn]
        outer = dot3(parts(left), parts(right), TN)
        held = 0.0
        if carried is not None:
            now = parts(carried)
            outer = outer + dot3(product, now)
            held = dot3(now, parts(q_ref[turn]))
        outer = even(outer)
        once = dot3(product, parts(outer))
        once_parts = parts(once)
        twice = dot3(product, once_parts) + 0.5 * dot3(once_parts, product)
        carried = even(held + 3.5 * once - 0.5 * twice) - 3.75 * outer
    return carried


def chains_kernel(sums_ref, grads_ref, kernel_ref, early_ref, late_ref, thin_ref, done_ref):
    kernel = kernel_ref[...]
    factors = [parts(early_ref[turn]) for turn in range(HALF)]
    factors += [parts(late_ref[turn]) for turn in range(PINV_ITERS - HALF)]
    right = sums_ref[:HD] / sums_ref[HD : HD + 1]
    left = dot3(parts(grads_ref[...]), parts(kernel), NT) * (1.0 / norm_of(kernel))
    for turn in range(PINV_ITERS):
        back = PINV_ITERS - 1 - turn
        thin_ref[turn] = left
        thin_ref[PINV_ITERS + back] = right
        left = dot3(parts(left), factors[turn])
        right = dot3(parts(right), factors[back])
    thin_ref[2 * PINV_ITERS] = right
    done_ref[...] = jnp.zeros_like(done_ref)


def pull_late_kernel(thin_ref, q_ref, p_ref, out_ref):
    out_ref[...] = pull_turns(None, PINV_ITERS - HALF, q_ref, p_ref, thin_ref, HALF)


def pull_early_kernel(carried_ref, marks_ref, grads_ref, kernel_ref, q_ref, p_ref, thin_ref, out_ref):
    marks = marks_ref[...]
    kernel = kernel_ref[...]
    scale = 1.0 / norm_of(kernel)
    halves = parts(kernel)
    grads = grads_ref[...]
    whole = parts(thin_ref[2 * PINV_ITERS])
    carried = pull_turns(carried_ref[...], HALF, q_ref, p_ref, thin_ref, 0)
    mixed = dot3(whole, halves) * scale
    grad_norm = -(total_of(grads * mixed) + total_of(carried * p_ref[0])) * scale
    grad_kernel = (
        dot3(whole, parts(grads), TN) * scale
        + (2.0 * scale) * dot3(parts(carried), halves)
        + 2.0 * grad_norm * kernel
    )
    grad_scores = kernel * (grad_kernel - jnp.sum(kernel * grad_kernel, axis=-1, keepdims=True))
    high, low = parts(grad_scores)
    out_ref[:HD] = dot(marks[HD:], high, NT) + dot(marks[HD:], low, NT)
    out_ref[HD:] = dot(marks[:HD], high) + dot(marks[:HD], low)


def ordered(kernel, count, inputs):
    def body(*refs):
        return kernel(*refs[: inputs - count], *refs[inputs:])

    return body


ANYWHERE = pl.BlockSpec(memory_space=pl.ANY)
WHOLE = pl.BlockSpec(memory_space=pltpu.VMEM)
SCALARS = pl.BlockSpec(memory_space=pltpu.SMEM)
STAY = pl.BlockSpec(memory_space=pltpu.HBM)


def call(kernel, outs, micros, room=ROOM, **grid):
    return pl.pallas_call(
        kernel,
        out_shape=outs,
        compiler_params=pltpu.CompilerParams(vmem_limit_bytes=room * 1024 * 1024),
        **grid,
        cost_estimate=pl.CostEstimate(
            flops=int(micros * 10**9), bytes_accessed=1024, transcendentals=0
        ),
    )


def inverse_early(marks, after):
    size = marks.shape[-1]
    stack = jax.ShapeDtypeStruct((HALF, size, size), F32)
    return call(
        ordered(inverse_early_kernel, 1, 2),
        (
            jax.ShapeDtypeStruct((size, size), F32),
            stack,
            stack,
            jax.ShapeDtypeStruct((2, size, size), F32),
            jax.ShapeDtypeStruct((8, 128), F32),
        ),
        0.1,
        room=MARK_ROOM,
        in_specs=[WHOLE, ANYWHERE],
    )(marks, after)


def inverse_late(carried, after):
    size = carried.shape[-1]
    stack = jax.ShapeDtypeStruct((PINV_ITERS - HALF, size, size), F32)
    return call(
        ordered(inverse_late_kernel, 1, 2),
        (jax.ShapeDtypeStruct((size, size), F32), stack, stack),
        0.1,
        room=MARK_ROOM,
        in_specs=[WHOLE, ANYWHERE],
    )(carried, after)


def mixed_marks_of(sums, inverse, after):
    return call(
        ordered(mixed_marks_kernel, 1, 3),
        jax.ShapeDtypeStruct((HD, sums.shape[1]), BF16),
        0.1,
        in_specs=[WHOLE] * 2 + [ANYWHERE],
    )(sums, inverse, after)


def grad_values_of(sums, grads, inverse, after):
    return call(
        ordered(grad_values_kernel, 1, 4),
        jax.ShapeDtypeStruct((HD + 16, sums.shape[1]), BF16),
        0.1,
        in_specs=[WHOLE] * 3 + [ANYWHERE],
    )(sums, grads, inverse, after)


def thin_chains(sums, grads, kernel, early, late):
    size = kernel.shape[-1]
    return call(
        chains_kernel,
        (
            jax.ShapeDtypeStruct((2 * PINV_ITERS + 1, HD, size), F32),
            jax.ShapeDtypeStruct((8, 128), F32),
        ),
        1,
        room=PULL_ROOM,
    )(sums, grads, kernel, early, late)


def landmark_pull(marks, grads, kernel, early, late, thin, after, later):
    size = kernel.shape[-1]
    carried = call(
        ordered(pull_late_kernel, 1, 4),
        jax.ShapeDtypeStruct((size, size), F32),
        PULL_MICROS,
        room=PULL_ROOM,
        in_specs=[WHOLE] * 3 + [ANYWHERE],
    )(thin, *late, after)
    return call(
        ordered(pull_early_kernel, len(later), 7 + len(later)),
        jax.ShapeDtypeStruct((2 * HD, size), F32),
        PULL_MICROS,
        room=PULL_ROOM,
        in_specs=[WHOLE] * 7 + [ANYWHERE] * len(later),
    )(carried, marks, grads, kernel, *early, thin, *later)


def finish_kernel(sums_ref, inverse_ref, counts_ref, out_ref):
    out_ref[...] = ((sums_ref[...] + inverse_ref[...]) / counts_ref[...]).astype(BF16)


def finish_marks(sums, inverse, counts, after):
    return call(
        ordered(finish_kernel, 1, 4),
        jax.ShapeDtypeStruct(sums.shape, BF16),
        0.5,
        in_specs=[WHOLE] * 3 + [ANYWHERE],
    )(sums, inverse, counts, after)


def fold_kernel(bit, scalars_ref, kept_ref, received_ref, out_kept_ref, out_sent_ref):
    value = kept_ref[...] + received_ref[...].astype(F32)
    half = value.shape[0] // 2
    own_first = scalars_ref[2 + bit] == 0
    first, second = value[:half], value[half:]
    out_kept_ref[...] = jnp.where(own_first, first, second)
    out_sent_ref[...] = jnp.where(own_first, second, first).astype(out_sent_ref.dtype)


def fold_halves(scalars, kept, received, bit, after, kind=BF16):
    shape = (kept.shape[0] // 2, kept.shape[1])
    return call(
        ordered(functools.partial(fold_kernel, bit), 1, 4),
        (jax.ShapeDtypeStruct(shape, F32), jax.ShapeDtypeStruct(shape, kind)),
        0.1,
        in_specs=[SCALARS, WHOLE, WHOLE, ANYWHERE],
    )(scalars, kept, received, after)


def add_kernel(first_ref, second_ref, out_ref):
    out_ref[...] = first_ref[...] + second_ref[...]


def add_four_kernel(kept_ref, beside_ref, near_ref, far_ref, out_ref):
    out_ref[...] = (kept_ref[...] + beside_ref[...]) + (near_ref[...] + far_ref[...])


def add_four(kept, beside, near, far, after):
    return call(
        ordered(add_four_kernel, len(after), 4 + len(after)),
        jax.ShapeDtypeStruct(kept.shape, kept.dtype),
        0.1,
        in_specs=[WHOLE] * 4 + [ANYWHERE] * len(after),
    )(kept, beside, near, far, *after)


def add_parts(first, second, after):
    return call(
        ordered(add_kernel, 1, 3),
        jax.ShapeDtypeStruct(first.shape, first.dtype),
        0.1,
        in_specs=[WHOLE, WHOLE, ANYWHERE],
    )(first, second, after)


def join_kernel(scalars_ref, own_ref, other_ref, out_ref):
    own, other = own_ref[...], other_ref[...]
    own_first = scalars_ref[3] == 0
    out_ref[0] = jnp.where(own_first, own, other)
    out_ref[1] = jnp.where(own_first, other, own)


def join_heads(scalars, own, other, after):
    return call(
        ordered(join_kernel, 1, 4),
        jax.ShapeDtypeStruct((2,) + own.shape, own.dtype),
        0.1,
        in_specs=[SCALARS, WHOLE, WHOLE, ANYWHERE],
    )(scalars, own, other, after)


def row_of(column):
    return jnp.broadcast_to(column, (column.shape[0], 128)).T[:1]


def column_of(row):
    return jnp.broadcast_to(row, (8, row.shape[1])).T[:, :1]


def segments_of(starts, scalars_ref, tokens, offset=0):
    size = starts.shape[1]
    starts = starts.astype(F32)
    lane = lax.broadcasted_iota(jnp.int32, (1, size), 1)
    last = scalars_ref[1].astype(F32)
    ends = jnp.where(lane == size - 1, last, pltpu.roll(starts, size - 1, 1))
    place = lax.broadcasted_iota(jnp.int32, (1, tokens), 1) + (scalars_ref[0] + offset)
    place = place.astype(F32)
    member = (place >= column_of(starts)) & (place < column_of(ends))
    return jnp.where(member, 1.0, 0.0).astype(BF16)


def full_kernel(kernels):
    channels = kernels.shape[1]
    large_part = kernels[0:49].reshape(7, 7, channels)
    middle_part = jnp.pad(kernels[49:74].reshape(5, 5, channels), ((1, 1), (1, 1), (0, 0)))
    small_part = jnp.pad(kernels[74:83].reshape(3, 3, channels), ((2, 2), (2, 2), (0, 0)))
    return large_part + middle_part + small_part


def lay_grid(scalars_ref, inner_ref, own_ref, outer_ref, padded_ref, shifted_ref):
    rows, cols, feats = shifted_ref.shape[1:]
    padded_ref[:, 0:8] = jnp.zeros((rows, 8, feats), F32)
    padded_ref[:, 8 + cols :] = jnp.zeros((rows, 8, feats), F32)

    def laid(value):
        return value.astype(F32).T.reshape(-1, cols, feats)

    before, after = in_order(scalars_ref, inner_ref[0], outer_ref[0])
    padded_ref[0:3, 8 : 8 + cols] = laid(before)
    padded_ref[3 : rows - 3, 8 : 8 + cols] = laid(own_ref[0])
    padded_ref[rows - 3 :, 8 : 8 + cols] = laid(after)
    for col in range(7):
        shifted_ref[col] = padded_ref[:, 5 + col : 5 + col + cols]


def back_kernel(scalars_ref, before_ref, own_ref, after_ref, taps_ref, out_ref, low_ref, sums_ref, padded_ref, shifted_ref, flat_ref):
    lay_grid(scalars_ref, before_ref, own_ref, after_ref, padded_ref, shifted_ref)
    rows, cols, feats = shifted_ref.shape[1:]

    def one_row(row, sums):
        centre = shifted_ref[3, row + 3]
        total = centre
        for col in range(7):
            for shift in range(7):
                tap = 48 - (shift * 7 + col)
                total = total + taps_ref[tap : tap + 1] * shifted_ref[col, row + shift]
        flat_ref[row] = total
        return (
            sums[0] + jnp.sum(total, axis=0, keepdims=True),
            sums[1] + jnp.sum(centre, axis=0, keepdims=True),
        )

    zero = jnp.zeros((1, feats), F32)
    sums = lax.fori_loop(0, rows - 6, one_row, (zero, zero))
    sums = jnp.concatenate([sums[0], sums[1], jnp.zeros((6, feats), F32)], axis=0)

    @pl.when(pl.program_id(0) == 0)
    def _():
        sums_ref[...] = sums

    @pl.when(pl.program_id(0) > 0)
    def _():
        sums_ref[...] += sums

    back = flat_ref[...].reshape(-1, feats).T
    out_ref[0] = back
    low_ref[0] = back.astype(BF16)


def kernel_grad_kernel(scalars_ref, inner_ref, own_ref, outer_ref, cot_ref, held_ref, grad_ref, padded_ref, shifted_ref, cot_grid_ref):
    lay_grid(scalars_ref, inner_ref, own_ref, outer_ref, padded_ref, shifted_ref)
    rows, cols, feats = shifted_ref.shape[1:]
    cot_grid_ref[...] = cot_ref[0].astype(F32).T.reshape(-1, cols, feats)
    grad_ref[...] = held_ref[...]

    def one_row(row, carried):
        cot = cot_grid_ref[row]
        for col in range(7):
            for shift in range(7):
                cells = cot * shifted_ref[col, row + shift]
                grad_ref[shift * 7 + col] += jnp.sum(cells.reshape(-1, 8, feats), axis=0)
        return carried

    lax.fori_loop(0, rows - 6, one_row, 0)


def mix_kernel(scalars_ref, inner_ref, own_ref, outer_ref, taps_ref, biases_ref, out_ref, padded_ref, shifted_ref, flat_ref):
    lay_grid(scalars_ref, inner_ref, own_ref, outer_ref, padded_ref, shifted_ref)
    rows, cols, feats = shifted_ref.shape[1:]
    bias = biases_ref[1:2] + biases_ref[2:3] + biases_ref[3:4]

    def one_row(row, carried):
        total = shifted_ref[3, row + 3] + bias
        for col in range(7):
            for shift in range(7):
                tap = shift * 7 + col
                total = total + taps_ref[tap : tap + 1] * shifted_ref[col, row + shift]
        flat_ref[row] = total
        return carried

    lax.fori_loop(0, rows - 6, one_row, 0)
    out_ref[0] = flat_ref[...].reshape(-1, feats).T.astype(BF16)


def grid_scratch(rows, cols, feats):
    return [
        pltpu.VMEM((rows + 6, cols + 16, feats), F32),
        pltpu.VMEM((7, rows + 6, cols, feats), F32),
        pltpu.VMEM((rows, cols, feats), F32),
    ]


def per_slide(shape):
    zeros = (0,) * (len(shape) - 1)
    return pl.BlockSpec((1,) + tuple(shape[1:]), lambda s: (s,) + zeros)


def whole_block(shape):
    zeros = (0,) * len(shape)
    return pl.BlockSpec(tuple(shape), lambda *_: zeros)


def grid_back(scalars, before, own, after, taps, cols, first):
    slides, feats, tokens = own.shape
    rows = tokens // cols
    return call(
        ordered(back_kernel, 1, 6),
        (
            jax.ShapeDtypeStruct(own.shape, F32),
            jax.ShapeDtypeStruct(own.shape, BF16),
            jax.ShapeDtypeStruct((8, feats), F32),
        ),
        8,
        room=GRID_ROOM,
        grid=(slides,),
        in_specs=[
            SCALARS,
            per_slide(before.shape),
            per_slide(own.shape),
            per_slide(after.shape),
            whole_block(taps.shape),
            ANYWHERE,
        ],
        out_specs=(per_slide(own.shape), per_slide(own.shape), whole_block((8, feats))),
        scratch_shapes=grid_scratch(rows, cols, feats),
    )(scalars, before, own, after, taps, first)


def one_slide(slide, shape):
    return pl.BlockSpec((1,) + tuple(shape[1:]), lambda i: (slide, 0, 0))


def grid_kernel_grad(scalars, inner, own, outer, cotangent, held, cols, slide):
    slides, feats, tokens = own.shape
    rows = tokens // cols
    return call(
        kernel_grad_kernel,
        jax.ShapeDtypeStruct(held.shape, F32),
        1,
        room=GRID_ROOM,
        grid=(1,),
        in_specs=[SCALARS]
        + [one_slide(slide, item.shape) for item in (inner, own, outer, cotangent)]
        + [whole_block(held.shape)],
        out_specs=whole_block(held.shape),
        scratch_shapes=grid_scratch(rows, cols, feats),
    )(scalars, inner, own, outer, cotangent, held)


def grid_mix(scalars, inner, own, outer, taps, biases, cols, slide, out=None):
    slides, feats, tokens = own.shape
    rows = tokens // cols
    kernel, extra, specs, aliases = mix_kernel, (), [], {}
    if out is not None:
        kernel, extra, specs, aliases = ordered(mix_kernel, 1, 7), (out,), [ANYWHERE], {6: 0}
    return call(
        kernel,
        jax.ShapeDtypeStruct(own.shape, BF16),
        1,
        room=GRID_ROOM,
        grid=(1,),
        in_specs=[SCALARS]
        + [one_slide(slide, item.shape) for item in (inner, own, outer)]
        + [whole_block(item.shape) for item in (taps, biases)]
        + specs,
        out_specs=one_slide(slide, own.shape),
        scratch_shapes=grid_scratch(rows, cols, feats),
        input_output_aliases=aliases,
    )(scalars, inner, own, outer, taps, biases, *extra)


def pack_kernel(sums_ref, bias_ref, lines_ref, conv_ref, out_ref):
    feats = sums_ref.shape[2]
    share = out_ref.shape[1] // feats
    out_ref[...] = jnp.zeros_like(out_ref)
    totals = jnp.sum(sums_ref[...], axis=1)
    for row in range(51):
        line = totals[row : row + 1] if row < 49 else bias_ref[row - 49 : row - 48]
        at = row % share * feats
        out_ref[row // share : row // share + 1, at : at + feats] = line
    for head in range(conv_ref.shape[0]):
        line = conv_ref[head, :, 0:1]
        line = jnp.concatenate([line, jnp.zeros((64 - line.shape[0], 1), F32)], axis=0)
        out_ref[CONV_ROW : CONV_ROW + 1, head * 64 : head * 64 + 64] = row_of(line)
    out_ref[NORM_ROW : NORM_ROW + 2] = lines_ref[0:2]


def pack_sums(sums, bias_sums, lines, conv, full):
    return call(pack_kernel, jax.ShapeDtypeStruct((SMALL, full), F32), 0.2)(
        sums, bias_sums, lines, conv
    )


def lay_line(before, rows, after, line_ref):
    tokens = rows.shape[1]
    width = line_ref.shape[1]
    line_ref[:, :REACH] = before
    line_ref[:, REACH : REACH + tokens] = rows
    line_ref[:, REACH + tokens : 2 * REACH + tokens] = after
    line_ref[:, 2 * REACH + tokens :] = jnp.zeros((HD, width - tokens - 2 * REACH), BF16)


def line_width(tokens):
    return (-(-tokens // 128) + 1) * 128


def pairs_of(ref):
    return [(s, h) for h in range(ref.shape[1]) for s in range(ref.shape[0])]


def band(line):
    wide = jnp.broadcast_to(line, (128, 256))
    return parts(pltpu.roll(wide, 0, 1, stride=1, stride_axis=0))


def line_conv(line_ref, bands, out_ref, at):
    tokens = out_ref.shape[-1]
    high, low = bands
    for begin in range(0, tokens, 128):
        width = min(128, tokens - begin)
        held = line_ref[:, begin : begin + 256]
        out = dot(held, high, NT) + dot(held, low, NT)
        out_ref[at[0], at[1], :, begin : begin + width] = out[:, :width].astype(out_ref.dtype)


def residual_kernel(scalars_ref, inner_ref, rows_ref, outer_ref, taps_ref, out_ref, done_ref, lines_ref):
    done_ref[...] = jnp.zeros_like(done_ref)
    for index, at in enumerate(pairs_of(rows_ref)):
        line_ref = lines_ref.at[index]
        before, after = in_order(scalars_ref, inner_ref[at], outer_ref[at])
        lay_line(before, rows_ref[at[0], at[1], 2 * HD :], after, line_ref)
        line_conv(line_ref, band(taps_ref[at[1]]), out_ref, at)


def back_line_kernel(
    scalars_ref, value_inner_ref, rows_ref, value_outer_ref, inner_ref, low_ref, outer_ref, taps_ref,
    out_ref, grad_ref, values_ref, lines_ref,
):
    tokens = out_ref.shape[-1]
    gap = lax.broadcasted_iota(jnp.int32, (128, 256), 1) - lax.broadcasted_iota(
        jnp.int32, (128, 256), 0
    )
    cross = jnp.zeros((128, 256), F32)
    for index, at in enumerate(pairs_of(rows_ref)):
        value_ref, line_ref = values_ref.at[index], lines_ref.at[index]
        rows = rows_ref[at[0], at[1], 2 * HD :]
        before, after = in_order(scalars_ref, value_inner_ref[at], value_outer_ref[at])
        lay_line(before, rows, after, value_ref)
        before, after = in_order(scalars_ref, inner_ref[at], outer_ref[at])
        lay_line(before, low_ref[at], after, line_ref)
        line_conv(line_ref, band(taps_ref[at[1]]), out_ref, at)
        for begin in range(0, tokens, 128):
            width = min(128, tokens - begin)
            lane = lax.broadcasted_iota(jnp.int32, (HD, 256), 1)
            inside = (lane >= REACH) & (lane < REACH + width)
            centre = line_ref[:, begin : begin + 256].astype(F32)
            centre = jnp.where(inside, centre, 0.0).astype(BF16)
            held = value_ref[:, begin : begin + 256]
            cross = cross + dot(centre, held, TN)[: 128 + REACH][REACH:]
        if at[0] == rows_ref.shape[0] - 1:
            lines = [
                jnp.sum(jnp.where(gap == tap, cross, 0.0), axis=0, keepdims=True)
                for tap in range(TAPS)
            ]
            lines.append(jnp.zeros((40 - TAPS, 256), F32))
            totals = jnp.sum(jnp.concatenate(lines, axis=0), axis=1, keepdims=True)
            grad_ref[at[1]] = jnp.broadcast_to(totals, (40, 128))
            cross = jnp.zeros((128, 256), F32)


def line_taps(conv_weight):
    return jnp.pad(conv_weight, ((0, 0), (0, 256 - TAPS)))[:, None, :]


def residual_of(scalars, before, rows, after, conv_weight):
    slides, heads, _, tokens = rows.shape
    return call(
        residual_kernel,
        (
            jax.ShapeDtypeStruct((slides, heads, HD, tokens), F32),
            jax.ShapeDtypeStruct((8, 128), F32),
        ),
        0.1,
        in_specs=[SCALARS] + [WHOLE] * 4,
        scratch_shapes=[pltpu.VMEM((slides * heads, HD, line_width(tokens)), BF16)],
    )(scalars, before, rows, after, line_taps(conv_weight))


def back_line(scalars, value_before, rows, value_after, before, low, after, conv_weight, later):
    slides, heads, _, tokens = rows.shape
    lines = pltpu.VMEM((slides * heads, HD, line_width(tokens)), BF16)
    return call(
        ordered(back_line_kernel, 1, 9),
        (
            jax.ShapeDtypeStruct((slides, heads, HD, tokens), BF16),
            jax.ShapeDtypeStruct((heads, 40, 128), F32),
        ),
        1,
        in_specs=[SCALARS] + [WHOLE] * 7 + [ANYWHERE],
        scratch_shapes=[lines, lines],
    )(scalars, value_before, rows, value_after, before, low, after, line_taps(conv_weight[:, ::-1]), later)


def put_halves(kept_ref, sent_ref, mine, sums):
    own_first = mine == 0
    for head, (first, second) in enumerate(zip(*sums)):
        kept_ref[head] = jnp.where(own_first, first, second)
        sent_ref[head] = jnp.where(own_first, second, first)


def all_blocks(shape):
    zeros = (0,) * (len(shape) - 2)
    return pl.BlockSpec((shape[0], 1) + tuple(shape[2:]), lambda s: (0, s) + zeros)


def norm_kernel(scalars_ref, gathered_ref, weight_ref, norm_ref, mask_ref, starts_ref, normed_ref, stats_ref, rows_ref, kept_ref, sent_ref, sums_ref):
    count, _, feats, tokens = gathered_ref.shape
    heads = rows_ref.shape[1]
    full = feats * count
    slide, chunk = pl.program_id(0), pl.program_id(1)
    total, squares = 0.0, 0.0
    for slot in range(count):
        cells = gathered_ref[slot, 0].astype(F32)
        total = total + jnp.sum(cells, axis=0, keepdims=True)
        squares = squares + jnp.sum(cells * cells, axis=0, keepdims=True)
    mean = total / full
    inv_std = lax.rsqrt(squares / full - mean * mean + EPS_NORM)
    stats_ref[0] = jnp.concatenate([mean, inv_std, jnp.zeros((6, tokens), F32)], axis=0)
    gain, bias = column_of(norm_ref[0:1]), column_of(norm_ref[1:2])
    for slot in range(count):
        span = slice(slot * feats, (slot + 1) * feats)
        centered = (gathered_ref[slot, 0].astype(F32) - mean) * inv_std
        normed_ref[0, span] = (centered * gain[span] + bias[span]).astype(BF16)
    normed = normed_ref[0]
    mask = mask_ref[slide, chunk].astype(F32)
    onehot = segments_of(starts_ref[pl.ds(slide, 1)], scalars_ref, tokens, chunk * tokens)
    counts = dot(jnp.broadcast_to(mask, (16, tokens)).astype(BF16), onehot, NT)[:8]
    own = scalars_ref[2] == slide
    fresh = chunk == 0
    for head in range(heads):
        row = head * 3 * HD
        projected = dot(weight_ref[row : row + 3 * HD], normed)
        rows_ref[0, head, :HD] = (projected[:HD] * mask * HD ** (-0.5)).astype(BF16)
        rows_ref[0, head, HD:] = (projected[HD:] * mask).astype(BF16)
        sums = dot(rows_ref[0, head, : 2 * HD], onehot, NT)
        sums = jnp.concatenate([sums, counts], axis=0) + jnp.where(fresh, 0.0, sums_ref[head])
        sums_ref[head] = sums
        kept_ref[head] = jnp.where(own, sums, kept_ref[head])
        sent_ref[head] = jnp.where(own, sent_ref[head], sums)


def norm_project(scalars, gathered, weight, norm_params, mask, starts, after):
    count, slides, feats, tokens = gathered.shape
    heads = weight.shape[0] // (3 * HD)
    width = 384 if tokens % 384 == 0 else tokens
    chunks = tokens // width
    mask = mask.reshape(slides, chunks, 1, width)
    half = jax.ShapeDtypeStruct((heads, 2 * HD + 8, starts.shape[1]), F32)
    return call(
        ordered(norm_kernel, len(after), 6 + len(after)),
        (
            jax.ShapeDtypeStruct((slides, count * feats, tokens), BF16),
            jax.ShapeDtypeStruct((slides, 8, tokens), F32),
            jax.ShapeDtypeStruct((slides, heads, 3 * HD, tokens), BF16),
            half,
            half,
        ),
        0.1,
        room=LARGE_ROOM,
        grid=(slides, chunks),
        in_specs=[
            SCALARS,
            pl.BlockSpec((count, 1, feats, width), lambda s, c: (0, s, 0, c)),
        ]
        + [whole_block(item.shape) for item in (weight, norm_params, mask, starts)]
        + [ANYWHERE] * len(after),
        out_specs=(
            pl.BlockSpec((1, count * feats, width), lambda s, c: (s, 0, c)),
            pl.BlockSpec((1, 8, width), lambda s, c: (s, 0, c)),
            pl.BlockSpec((1, heads, 3 * HD, width), lambda s, c: (s, 0, 0, c)),
            whole_block(half.shape),
            whole_block(half.shape),
        ),
        scratch_shapes=[pltpu.VMEM(half.shape, F32)],
    )(scalars, gathered, weight, norm_params, mask, starts, *after)


def low_kernel(scalars_ref, far_ref, weight_ref, far_kernel_ref, low_ref, kept_ref, sent_ref, near_ref, kernel_ref, sem, kernel_sem):
    count, slides, feats, tokens = far_ref.shape
    heads = low_ref.shape[1]
    rows, kernels = [], []
    for s in range(slides):
        rows.append(
            [
                pltpu.make_async_copy(far_ref.at[slot, s], near_ref.at[slot, s], sem.at[slot, s])
                for slot in range(count)
            ]
        )
        kernels.append(
            pltpu.make_async_copy(far_kernel_ref.at[s], kernel_ref.at[s], kernel_sem.at[s])
        )
    for s in range(slides):
        for copy in rows[s] + [kernels[s]]:
            copy.start()
    sums = [[None] * heads for _ in range(slides)]
    for s in range(slides):
        for copy in rows[s]:
            copy.wait()
        low = dot(weight_ref[...], near_ref[:, s].reshape(count * feats, tokens)).astype(BF16)
        for head in range(heads):
            low_ref[s, head] = low[head * HD : (head + 1) * HD]
        kernels[s].wait()
        for head in range(heads):
            sums[s][head] = dot(low_ref[s, head], kernel_ref[s, head], NT)
    put_halves(kept_ref, sent_ref, scalars_ref[2], sums)


def head_gradient(scalars, gathered, weight, kernel, after):
    count, slides, feats, tokens = gathered.shape
    heads = feats // HD
    half = jax.ShapeDtypeStruct((heads, HD, kernel.shape[2]), F32)
    return call(
        ordered(low_kernel, 1, 5),
        (jax.ShapeDtypeStruct((slides, heads, HD, tokens), BF16), half, half),
        0.1,
        room=LARGE_ROOM,
        in_specs=[SCALARS, STAY, WHOLE, STAY, ANYWHERE],
        scratch_shapes=[
            pltpu.VMEM(gathered.shape, BF16),
            pltpu.VMEM(kernel.shape, BF16),
            pltpu.SemaphoreType.DMA((count, slides)),
            pltpu.SemaphoreType.DMA((slides,)),
        ],
    )(scalars, gathered, weight, kernel, after)


def section_kernel(gathered_ref, weight_ref, patch_ref, biases_ref, out_ref):
    count, slides, feats, tokens = gathered_ref.shape
    bias = column_of(biases_ref[0:1])
    for s in range(slides):
        branch = dot(weight_ref[...], gathered_ref[:, s].reshape(count * feats, tokens), TN)
        out_ref[s] = patch_ref[s].astype(F32) + branch + bias


def section(gathered, weight, patches, biases):
    return call(section_kernel, jax.ShapeDtypeStruct(patches.shape, F32), 1)(
        gathered, weight, patches, biases
    )


def final_kernel(grad_ref, gain_ref, stats_ref, table_ref, patch_ref, back_ref, out_ref):
    slides, feats, tokens = out_ref.shape
    full = table_ref.shape[1]
    gain = column_of(gain_ref[...])
    lines = {}
    for s, which, row, begin, end in line_pieces(slides, tokens, full):
        lines.setdefault((s, which), []).append(table_ref[row : row + 1, : end - begin])
    for s in range(slides):
        mean, inv_std = stats_ref[s, 0:1], stats_ref[s, 1:2]
        first, second = (jnp.concatenate(lines[s, which], axis=1) / full for which in range(2))
        centered = (patch_ref[s].astype(F32) - mean) * inv_std
        grad = grad_ref[s].astype(F32) * gain - first - centered * second
        out_ref[s] = inv_std * grad + back_ref[s]


def token_probs(marks, queries):
    scores = dot(marks[HD:], queries, TN)
    raised = jnp.exp(scores - jnp.max(scores, axis=0, keepdims=True))
    return raised * (1.0 / jnp.sum(raised, axis=0, keepdims=True))


def token_weights(marks, keys, mask):
    return jnp.exp(dot(marks[:HD], keys, TN)) * mask


def framed(values):
    return jnp.concatenate([values, jnp.ones((16, values.shape[1]), BF16)], axis=0)


def forward_kernel(scalars_ref, rows_ref, marks_ref, mask_ref, kernel_ref, kept_ref, sent_ref):
    sums = [[None] * rows_ref.shape[1] for _ in range(rows_ref.shape[0])]
    for at in pairs_of(rows_ref):
        rows, marks = rows_ref[at], marks_ref[at]
        weights = token_weights(marks, rows[HD : 2 * HD], mask_ref[at[0] : at[0] + 1].astype(F32)).astype(BF16)
        sums[at[0]][at[1]] = dot(framed(rows[2 * HD :]), weights, NT)[: HD + 8]
        kernel_ref[at] = token_probs(marks, rows[:HD]).astype(BF16)
    put_halves(kept_ref, sent_ref, scalars_ref[2], sums)


def mixed_kernel(pack_ref, kernel_ref, residual_ref, out_ref):
    for s, h in pairs_of(pack_ref):
        attended = dot(pack_ref[s, h], kernel_ref[s, h])
        out_ref[s, h * HD : (h + 1) * HD] = (attended + residual_ref[s, h]).astype(BF16)


def pull_one_kernel(rows_ref, marks_ref, pack_ref, low_ref, grads_ref, sums_ref):
    for at in pairs_of(rows_ref):
        queries, marks = rows_ref[at[0], at[1], :HD], marks_ref[at]
        probs = token_probs(marks, queries)
        pulled = probs * dot(pack_ref[at], low_ref[at], TN)
        grad_scores = (pulled - probs * jnp.sum(pulled, axis=0, keepdims=True)).astype(BF16)
        grads_ref[at] = dot(marks[HD:], grad_scores).astype(BF16)
        sums_ref[at] = dot(queries, grad_scores, NT)


def pull_three_kernel(scalars_ref, rows_ref, marks_ref, pack_ref, mask_ref, other_ref, grads_ref, value_ref, kept_ref, sent_ref):
    sums = [[None] * rows_ref.shape[1] for _ in range(rows_ref.shape[0])]
    for at in pairs_of(rows_ref):
        rows, marks, pack = rows_ref[at], marks_ref[at], pack_ref[at]
        keys = rows[HD : 2 * HD]
        raised = token_weights(marks, keys, mask_ref[at[0] : at[0] + 1].astype(F32))
        grad_three = (dot(pack, framed(rows[2 * HD :]), TN) * raised).astype(BF16)
        own = dot(keys, grad_three, NT)
        sums[at[0]][at[1]] = jnp.concatenate([own, other_ref[at]], axis=0)
        grads_ref[at] = dot(marks[:HD], grad_three).astype(BF16)
        value_ref[at] = dot(pack[:HD], raised.astype(BF16)).astype(BF16)
    put_halves(kept_ref, sent_ref, scalars_ref[2], sums)


def token_forward(scalars, rows, marks, mask, after):
    slides, heads, _, tokens = rows.shape
    size = marks.shape[-1]
    half = jax.ShapeDtypeStruct((heads, HD + 8, size), F32)
    return call(
        ordered(forward_kernel, 1, 5),
        (jax.ShapeDtypeStruct((slides, heads, size, tokens), BF16), half, half),
        0.1,
        in_specs=[SCALARS] + [WHOLE] * 3 + [ANYWHERE],
    )(scalars, rows, marks, mask, after)


def mixed_heads(pack, kernel, residual, after):
    slides, heads, size, tokens = kernel.shape
    return call(
        ordered(mixed_kernel, 1, 4),
        jax.ShapeDtypeStruct((slides, heads * HD, tokens), BF16),
        0.1,
        in_specs=[WHOLE] * 3 + [ANYWHERE],
    )(pack, kernel, residual, after)


def pull_one(rows, marks, pack, low, after):
    slides, heads, _, tokens = rows.shape
    return call(
        ordered(pull_one_kernel, 1, 5),
        (
            jax.ShapeDtypeStruct((slides, heads, HD, tokens), BF16),
            jax.ShapeDtypeStruct((slides, heads, HD, marks.shape[-1]), F32),
        ),
        1,
        in_specs=[WHOLE] * 4 + [ANYWHERE],
    )(rows, marks, pack, low, after)


def pull_three(scalars, rows, marks, pack, mask, other, after):
    slides, heads, _, tokens = rows.shape
    half = jax.ShapeDtypeStruct((heads, 2 * HD, marks.shape[-1]), F32)
    token = jax.ShapeDtypeStruct((slides, heads, HD, tokens), BF16)
    return call(
        ordered(pull_three_kernel, 1, 7),
        (token, token, half, half),
        1,
        in_specs=[SCALARS] + [WHOLE] * 5 + [STAY],
    )(scalars, rows, marks, pack, mask, other, after)


def project_kernel(scalars_ref, query_ref, key_ref, value_ref, line_ref, marks_ref, mask_ref, starts_ref, weight_ref, gathered_ref, normed_ref, stats_ref, norm_ref, out_rows_ref, low_ref, near_ref, moments_ref, lines_ref, kept_ref, sent_ref, rows_ref, sums_ref):
    count, slides, feats, tokens = gathered_ref.shape
    heads = query_ref.shape[1]
    gains = column_of(norm_ref[0:1])
    norms = [[0.0, 0.0] for _ in range(count)]
    for s in range(slides):
        mask = mask_ref[s : s + 1].astype(F32)
        onehot = segments_of(starts_ref[s : s + 1], scalars_ref, tokens)
        for head in range(heads):
            row = head * 3 * HD
            spread = dot(marks_ref[s, head], onehot)
            query = (query_ref[s, head].astype(F32) + spread[:HD]).astype(BF16).astype(F32) * mask
            key = (key_ref[s, head].astype(F32) + spread[HD:]).astype(BF16).astype(F32) * mask
            value = (value_ref[s, head].astype(F32) + line_ref[s, head].astype(F32)).astype(BF16)
            rows_ref[s, row : row + HD] = (query * HD ** (-0.5)).astype(BF16)
            rows_ref[s, row + HD : row + 2 * HD] = key.astype(BF16)
            rows_ref[s, row + 2 * HD : row + 3 * HD] = (value.astype(F32) * mask).astype(BF16)
        rows = rows_ref[s]
        mean, inv_std = stats_ref[s, 0:1], stats_ref[s, 1:2]
        first, second = 0.0, 0.0
        for slot in range(count):
            span = slice(slot * feats, (slot + 1) * feats)
            grad = dot(weight_ref[:, span], rows, TN)
            near_ref[slot, s] = grad.astype(BF16)
            centered = (gathered_ref[slot, s].astype(F32) - mean) * inv_std
            pulled = grad * centered
            gain = gains[span]
            first = first + jnp.sum(grad * gain, axis=0, keepdims=True)
            second = second + jnp.sum(pulled * gain, axis=0, keepdims=True)
            norms[slot][0] += jnp.sum(pulled, axis=1, keepdims=True)
            norms[slot][1] += jnp.sum(grad, axis=1, keepdims=True)
        moments_ref[s] = jnp.concatenate([first, second], axis=0)
    qkv_grad = 0.0
    out_grads = [0.0] * count
    for s in range(slides):
        qkv_grad = qkv_grad + dot(rows_ref[s], normed_ref[s], NT)
        for slot in range(count):
            out_grads[slot] += dot(out_rows_ref[s], low_ref[slot, s], NT)
    lines_ref[...] = jnp.zeros_like(lines_ref)
    sums_ref[: 3 * feats] = qkv_grad
    for slot in range(count):
        span = slice(slot * feats, (slot + 1) * feats)
        sums_ref[3 * feats : 4 * feats, span] = out_grads[slot]
        for line in range(2):
            lines_ref[line : line + 1, span] = row_of(norms[slot][line])
    half = sums_ref.shape[0] // 2
    own_first = scalars_ref[2] == 0
    first, second = sums_ref[:half], sums_ref[half:]
    kept_ref[...] = jnp.where(own_first, first, second)
    sent_ref[...] = jnp.where(own_first, second, first).astype(BF16)


def project_back(scalars, query, key, value, line, marks, mask, starts, weight, gathered, normed, stats, norm_params, heads_out, low):
    count, slides, feats, tokens = gathered.shape
    held = (query, key, value, line, marks, mask, starts, weight, gathered, normed, stats, norm_params, heads_out, low)
    return call(
        project_kernel,
        (
            jax.ShapeDtypeStruct((count, slides, feats, tokens), BF16),
            jax.ShapeDtypeStruct((slides, 2, tokens), F32),
            jax.ShapeDtypeStruct((8, count * feats), F32),
            jax.ShapeDtypeStruct((2 * feats, count * feats), F32),
            jax.ShapeDtypeStruct((2 * feats, count * feats), BF16),
        ),
        7,
        in_specs=[SCALARS] + [WHOLE] * len(held),
        scratch_shapes=[
            pltpu.VMEM((slides, weight.shape[0], tokens), BF16),
            pltpu.VMEM((4 * feats, count * feats), F32),
        ],
    )(scalars, *held)


DECAY = 1.0 - STEP ** (-0.8)


def second_of(old, grad):
    return DECAY * old + (1.0 - DECAY) * (grad * grad + EPS_FACTOR)


def shrink(update, usq_sum, weight_sq, entries):
    clip_factor = jnp.maximum(1.0, jnp.sqrt(usq_sum / entries))
    return RATE * jnp.sqrt(weight_sq / entries) * update / clip_factor


def scalar_line(values):
    lane = lax.broadcasted_iota(jnp.int32, (1, 128), 1)
    line = jnp.zeros((1, 128), F32)
    for index, value in values:
        line = jnp.where(lane == index, value, line)
    return line


def block_masks(shape):
    row = lax.broadcasted_iota(jnp.int32, shape, 0)
    return [jnp.where((row >= low) & (row < high), 1.0, 0.0) for low, high in BLOCKS]


def squares_kernel(qkv_ref, out_ref, biases_ref, kernels_ref, conv_ref, line_ref):
    def square(ref):
        value = ref[...]
        return value * value

    biases = square(biases_ref)
    kernels = square(kernels_ref)
    values = [(1, total_of(square(qkv_ref))), (3, total_of(square(out_ref)))]
    values.append((5, total_of(square(conv_ref))))
    values += [(7 + 2 * row, total_of(biases[row : row + 1])) for row in range(4)]
    masks = block_masks(kernels.shape)
    values += [(15 + 2 * block, total_of(kernels * mask)) for block, mask in enumerate(masks)]
    line_ref[...] = jnp.broadcast_to(scalar_line(values), line_ref.shape)


def weight_squares(*weights):
    return call(squares_kernel, jax.ShapeDtypeStruct((8, 128), F32), 2, room=LARGE_ROOM)(*weights)


def weight_grad(sums_ref, feats, index):
    return sums_ref[3 * feats * index : 3 * feats + feats * index].astype(F32)


def conv_grad_of(part_ref, heads):
    row = part_ref[CONV_ROW : CONV_ROW + 1]
    return jnp.concatenate([row[:, 64 * head : 64 * head + TAPS] for head in range(heads)], axis=0)


def part_row(part_ref, feats, row):
    share = part_ref.shape[1] // feats
    at = row % share * feats
    return part_ref[row // share : row // share + 1, at : at + feats]


def lay_bias_grad(part_ref, out_ref):
    feats = out_ref.shape[1]
    for row in range(4):
        out_ref[row : row + 1] = part_row(part_ref, feats, 49 + min(row, 1))


def lay_kernel_grad(part_ref, out_ref):
    feats = out_ref.shape[1]
    taps = list(range(49))
    taps += [7 * row + col for row in range(1, 6) for col in range(1, 6)]
    taps += [7 * row + col for row in range(2, 5) for col in range(2, 5)]
    for row, tap in enumerate(taps):
        out_ref[row : row + 1] = part_row(part_ref, feats, tap)


def rows_new_of(grad, rows):
    mean = jnp.sum(grad * grad, axis=1, keepdims=True) / grad.shape[1]
    return DECAY * column_of(rows) + (1.0 - DECAY) * (mean + EPS_FACTOR)


def line_pieces(slides, tokens, full):
    share = -(-tokens // full)
    return [
        (s, which, 8 + (2 * s + which) * share + piece, piece * full, min(tokens, (piece + 1) * full))
        for s in range(slides)
        for which in range(2)
        for piece in range(share)
    ]


def table_kernel(sums_ref, part_ref, qkv_rows_ref, out_rows_ref, bias_second_ref, kernel_second_ref, conv_second_ref, line_ref, moments_ref, table_ref, bias_ref, kernel_ref):
    feats = bias_second_ref.shape[1]
    heads = conv_second_ref.shape[0]
    values = []
    table_ref[...] = jnp.zeros_like(table_ref)
    for index, rows_ref in enumerate((qkv_rows_ref, out_rows_ref)):
        grad = weight_grad(sums_ref, feats, index)
        squares = grad * grad
        rows_new = rows_new_of(grad, rows_ref[...])
        table_ref[2 * index : 2 * index + 1] = jnp.sum(squares, axis=0, keepdims=True)
        table_ref[2 * index + 1 : 2 * index + 2] = jnp.sum(
            squares * (1.0 / rows_new), axis=0, keepdims=True
        )
        values.append((2 * index, total_of(rows_new)))
    table_ref[4:6] = part_ref[NORM_ROW : NORM_ROW + 2]

    def update_squares(grad, second):
        return grad * grad / second_of(second, grad)

    conv_grad = conv_grad_of(part_ref, heads)
    values.append((4, total_of(update_squares(conv_grad, conv_second_ref[...]))))
    lay_bias_grad(part_ref, bias_ref)
    bias_squares = update_squares(bias_ref[...], bias_second_ref[...])
    values += [(6 + 2 * row, total_of(bias_squares[row : row + 1])) for row in range(4)]
    lay_kernel_grad(part_ref, kernel_ref)
    kernel_squares = update_squares(kernel_ref[...], kernel_second_ref[...])
    masks = block_masks(kernel_squares.shape)
    values += [
        (14 + 2 * block, total_of(kernel_squares * mask)) for block, mask in enumerate(masks)
    ]
    table_ref[6:7, :128] = scalar_line(values) + line_ref[0:1]
    slides, _, tokens = moments_ref.shape
    for s, which, row, begin, end in line_pieces(slides, tokens, table_ref.shape[1]):
        table_ref[row : row + 1, : end - begin] = moments_ref[s, which : which + 1, begin:end]


def optimizer_table(gradients, rows, seconds, line, moments):
    full = gradients[0].shape[1]
    lines = len(line_pieces(moments.shape[0], moments.shape[2], full))
    return call(
        table_kernel,
        jax.ShapeDtypeStruct((8 + -(-lines // 8) * 8, full), F32),
        0.2,
        scratch_shapes=[pltpu.VMEM(seconds[0].shape, F32), pltpu.VMEM(seconds[1].shape, F32)],
    )(*gradients, *rows, *seconds, line, moments)


def state_kernel(sums_ref, part_ref, qkv_rows_ref, out_rows_ref, bias_second_ref, kernel_second_ref, conv_second_ref, qkv_grad_ref, out_grad_ref, bias_grad_ref, kernel_grad_ref, conv_grad_ref, qkv_rows_new_ref, out_rows_new_ref, bias_new_ref, kernel_new_ref, conv_new_ref):
    feats = bias_second_ref.shape[1]
    heads = conv_second_ref.shape[0]
    for index, (rows_ref, grad_ref, rows_new_ref) in enumerate(
        (
            (qkv_rows_ref, qkv_grad_ref, qkv_rows_new_ref),
            (out_rows_ref, out_grad_ref, out_rows_new_ref),
        )
    ):
        grad = weight_grad(sums_ref, feats, index)
        grad_ref[...] = grad
        rows_new_ref[...] = row_of(rows_new_of(grad, rows_ref[...]))
    conv_grad_ref[...] = conv_grad_of(part_ref, heads)
    lay_bias_grad(part_ref, bias_grad_ref)
    lay_kernel_grad(part_ref, kernel_grad_ref)
    conv_new_ref[...] = second_of(conv_second_ref[...], conv_grad_ref[...])
    bias_new_ref[...] = second_of(bias_second_ref[...], bias_grad_ref[...])
    kernel_new_ref[...] = second_of(kernel_second_ref[...], kernel_grad_ref[...])


def optimizer_state(gradients, rows, seconds, weights, after):
    return call(
        ordered(state_kernel, 1, 8),
        tuple(like(item) for item in weights + rows + seconds),
        0.2,
        room=LARGE_ROOM,
        in_specs=[WHOLE] * 7 + [ANYWHERE],
    )(*gradients, *rows, *seconds, after)


def step_kernel(
    table_ref,
    sums_ref,
    part_ref,
    qkv_rows_ref,
    out_rows_ref,
    bias_second_ref,
    kernel_second_ref,
    conv_second_ref,
    qkv_cols_ref,
    out_cols_ref,
    norm_second_ref,
    norm_ref,
    qkv_weight_ref,
    out_weight_ref,
    biases_ref,
    kernels_ref,
    conv_weight_ref,
    norm_grad_ref,
    qkv_cols_new_ref,
    out_cols_new_ref,
    norm_second_new_ref,
    qkv_new_ref,
    out_new_ref,
    norm_new_ref,
    bias_new_ref,
    kernel_new_ref,
    conv_new_ref,
):
    feats, full = out_weight_ref.shape
    heads = conv_weight_ref.shape[0]

    def scalar(index):
        return table_ref[6:7, index : index + 1]

    for index, (rows, cols_ref, cols_new_ref, rows_ref, weight_ref, new_ref) in enumerate(
        (
            (3 * full, qkv_cols_ref, qkv_cols_new_ref, qkv_rows_ref, qkv_weight_ref, qkv_new_ref),
            (full, out_cols_ref, out_cols_new_ref, out_rows_ref, out_weight_ref, out_new_ref),
        )
    ):
        mean = scalar(2 * index) / rows
        cols = DECAY * cols_ref[...] + (1.0 - DECAY) * (
            table_ref[2 * index : 2 * index + 1] / rows + EPS_FACTOR
        )
        cols_new_ref[...] = cols
        usq = mean * total_of(table_ref[2 * index + 1 : 2 * index + 2] / cols)
        grad = weight_grad(sums_ref, feats, index)
        update = grad * lax.rsqrt(rows_new_of(grad, rows_ref[...]) * cols / mean)
        new_ref[...] = weight_ref[...] - shrink(update, usq, scalar(2 * index + 1), rows * full)

    norm_grad = table_ref[4:6]
    norm_grad_ref[...] = norm_grad
    norm_second = second_of(norm_second_ref[...], norm_grad)
    norm_second_new_ref[...] = norm_second
    update = norm_grad * lax.rsqrt(norm_second)
    norm = norm_ref[...]
    norm_new_ref[...] = norm - shrink(
        update,
        jnp.sum(update * update, axis=1, keepdims=True),
        jnp.sum(norm * norm, axis=1, keepdims=True),
        full,
    )

    conv_grad = conv_grad_of(part_ref, heads)
    conv_update = conv_grad * lax.rsqrt(second_of(conv_second_ref[...], conv_grad))
    conv_new_ref[...] = conv_weight_ref[...] - shrink(
        conv_update, scalar(4), scalar(5), HEADS * TAPS
    )
    lay_bias_grad(part_ref, bias_new_ref)
    bias_grad = bias_new_ref[...]
    bias_update = bias_grad * lax.rsqrt(second_of(bias_second_ref[...], bias_grad))
    for row in range(4):
        at = slice(row, row + 1)
        bias_new_ref[at] = biases_ref[at] - shrink(
            bias_update[at], scalar(6 + 2 * row), scalar(7 + 2 * row), full
        )
    lay_kernel_grad(part_ref, kernel_new_ref)
    kernel_grad = kernel_new_ref[...]
    kernel_update = kernel_grad * lax.rsqrt(second_of(kernel_second_ref[...], kernel_grad))
    usq, wsq, entries = 0.0, 0.0, 0.0
    masks = block_masks(kernel_grad.shape)
    for index, (low, high) in enumerate(BLOCKS):
        usq = usq + masks[index] * scalar(14 + 2 * index)
        wsq = wsq + masks[index] * scalar(15 + 2 * index)
        entries = entries + masks[index] * ((high - low) * full)
    kernel_new_ref[...] = kernels_ref[...] - shrink(kernel_update, usq, wsq, entries)


def last_kernel(inputs, outputs, *refs):
    split = inputs + outputs
    step_kernel(*refs[:inputs], *refs[inputs + 5 : split + 5])
    table_ref, patch_ref = refs[0], refs[split + 5]
    grad_ref, gain_ref, stats_ref, patches_ref, back_ref = refs[inputs : inputs + 5]
    final_kernel(grad_ref, gain_ref, stats_ref, table_ref, patches_ref, back_ref, patch_ref)


def optimizer_step(table, gradients, rows, seconds, cols, norm_params, weights, patch, after):
    held = (table,) + gradients + rows + seconds + cols + (norm_params,) + weights
    outs = (norm_params,) + cols + weights[:2] + (norm_params,) + weights[2:]
    patch_out = jax.ShapeDtypeStruct(patch[3].shape, F32)
    total = len(held) + len(patch)
    return call(
        ordered(functools.partial(last_kernel, len(held), len(outs)), 1, total + 1),
        tuple(like(item) for item in outs) + (patch_out,),
        0.2,
        room=LARGE_ROOM,
        in_specs=[WHOLE] * total + [ANYWHERE],
    )(*held, *patch, after)


def like(value):
    return jax.ShapeDtypeStruct(value.shape, value.dtype)


def local(
    patches,
    hole_mask,
    seg_start,
    cotangent,
    qkv_weight,
    out_weight,
    norm_params,
    biases,
    kernels,
    conv_weight,
    qkv_rows,
    qkv_cols,
    out_rows,
    out_cols,
    norm_second,
    bias_second,
    kernel_second,
    conv_second,
):
    patch_count = lax.axis_size("patch")
    head_count = lax.axis_size("head")
    patch_index = lax.axis_index("patch")
    head_index = lax.axis_index("head")
    slide_count, feat_width, tokens_dev = patches.shape
    heads = feat_width // HD
    full_width = feat_width * head_count
    total_tokens = tokens_dev * patch_count
    grid_cols = math.isqrt(total_tokens)
    offset = head_index * feat_width
    halo = 3 * grid_cols

    scalars = jnp.stack(
        [patch_index * tokens_dev, jnp.int32(total_tokens)]
        + [bit_of("patch", bit) for bit in range((patch_count - 1).bit_length())]
    )

    gathered = lax.all_gather(patches, "head")

    out_low = out_weight.astype(BF16)
    out_blocks = [lax.dynamic_slice_in_dim(out_low, offset, feat_width, 1)]
    for hop in range(1, head_count):
        block = lax.dynamic_slice_in_dim(
            out_low, ((head_index + hop) % head_count) * feat_width, feat_width, 1
        )
        out_blocks.append(
            lax.ppermute(block, "head", [(i, (i + hop) % head_count) for i in range(head_count)])
        )
    out_blocks = jnp.stack(out_blocks)
    out_own = jnp.concatenate(
        [
            lax.dynamic_index_in_dim(out_blocks, (head_index - z) % head_count, 0, keepdims=False)
            for z in range(head_count)
        ]
    )

    cot_before, cot_after = neighbours(cotangent, halo)
    taps = full_kernel(kernels).reshape(49, feat_width)
    back_flat, grad_low, bias_part = grid_back(scalars, cot_before, cotangent, cot_after, taps, grid_cols, out_own)
    grad_all = lax.all_gather(grad_low, "head")

    qkv_low = qkv_weight.astype(BF16)
    scalars_row = jnp.zeros((8, 128), F32)
    weight_sums = weight_squares(qkv_weight, out_weight, biases, kernels, conv_weight)

    normed, stats, rows, *mark_sums = norm_project(
        scalars,
        gathered,
        qkv_low,
        norm_params,
        hole_mask,
        seg_start,
        (grad_low, out_own, weight_sums),
    )
    value_before, value_after = neighbours(rows[:, :, 2 * HD :], REACH)
    own_sums = sum_to_owner(scalars, *mark_sums, direct=(value_before, value_after))
    own_counts = own_sums[2 * HD : 2 * HD + 1]
    own_marks = (own_sums[: 2 * HD] / own_counts).astype(BF16)
    residual, residual_done = residual_of(scalars, value_before, rows, value_after, conv_weight)
    marks = from_owner(own_marks, heads, scalars, residual_done)

    kernel_one, *value_parts = token_forward(scalars, rows, marks, hole_mask, residual_done)
    own_kernel, *own_early, own_carried, early_done = inverse_early(own_marks, value_parts[0])
    own_inverse_z, *own_late = inverse_late(own_carried, own_marks)
    own_values = sum_to_owner(scalars, *value_parts, after=early_done)
    own_mixed = mixed_marks_of(own_values, own_inverse_z, residual_done)
    mixed_marks = from_owner(own_mixed, heads, scalars, scalars_row)

    head_low, *mixed_parts = head_gradient(scalars, grad_all, out_low, kernel_one, own_values)
    heads_out = mixed_heads(mixed_marks, kernel_one, residual, mixed_parts[0])
    heads_all = lax.all_gather(heads_out, "head")
    own_grad_mixed = sum_to_owner(scalars, *mixed_parts)
    low_before, low_after = neighbours(head_low, REACH)
    query_grads, key_mark_parts = pull_one(rows, marks, mixed_marks, head_low, heads_out)
    own_pack = grad_values_of(own_values, own_grad_mixed, own_inverse_z, key_mark_parts)
    own_thin, thin_done = thin_chains(own_values, own_grad_mixed, own_kernel, own_early[0], own_late[0])

    pack = from_owner(own_pack, heads, scalars, thin_done)
    key_grads, value_grads, *mark_parts = pull_three(
        scalars, rows, marks, pack, hole_mask, key_mark_parts, scalars_row
    )
    own_grads = sum_to_owner(scalars, *mark_parts)
    own_inverse = landmark_pull(
        own_marks, own_grad_mixed, own_kernel, own_early, own_late, own_thin, mark_parts[0], (low_before, low_after)
    )
    own_mark_grads = finish_marks(own_grads, own_inverse, own_counts, own_counts)
    value_from_conv, conv_lines = back_line(
        scalars, value_before, rows, value_after, low_before, head_low, low_after, conv_weight, own_mark_grads
    )
    mark_grads = from_owner(own_mark_grads, heads, scalars, conv_lines)

    grad_normed, moments, lines, *sums = project_back(
        scalars,
        query_grads,
        key_grads,
        value_grads,
        value_from_conv,
        mark_grads,
        hole_mask,
        seg_start,
        qkv_low,
        gathered,
        normed,
        stats,
        norm_params,
        heads_out,
        grad_all,
    )
    section_one = section(heads_all, out_own, patches, biases)
    sec_before, sec_after = neighbours(section_one, halo)
    own_grad = lax.psum_scatter(grad_normed, "head", scatter_dimension=0, tiled=True)[0]

    block_out, held, grads = None, jnp.zeros((49, 8, feat_width), F32), []
    grid_args = (scalars, sec_before, section_one, sec_after)
    for slide in range(slide_count):
        held = grid_kernel_grad(*grid_args, cotangent, held, grid_cols, slide)
        block_out = grid_mix(*grid_args, taps, biases, grid_cols, slide, block_out)
        grads.append(held)
    kernel_part = pack_sums(held, bias_part, lines, conv_lines, full_width)

    sums, part = sum_rows(scalars, *sums, kernel_part, "patch", (section_one, grads[0]))

    gradients = (sums, part)
    rows_old = (qkv_rows[None, :], out_rows[None, :])
    seconds = (bias_second, kernel_second, conv_second)
    table = optimizer_table(gradients, rows_old, seconds, weight_sums, moments)
    gain_own = lax.dynamic_slice_in_dim(norm_params, offset, feat_width, 1)[0:1]
    weights = (qkv_weight, out_weight, biases, kernels, conv_weight)
    emitted = optimizer_state(gradients, rows_old, seconds, weights, table)
    qkv_grad, out_grad, bias_grad, kernel_grad, conv_grad = emitted[:5]
    qkv_rows_new, out_rows_new, bias_second_new, kernel_second_new, conv_second_new = emitted[5:]
    table = all_sum(table, "head")
    cols = (qkv_cols[None, :], out_cols[None, :], norm_second)
    norm_grad, qkv_cols_new, out_cols_new, norm_second_new, *news = optimizer_step(
        table,
        gradients,
        rows_old,
        seconds,
        cols,
        norm_params,
        weights,
        (own_grad, gain_own, stats, patches, back_flat),
        emitted[9],
    )
    qkv_new, out_new, norm_new, bias_new, kernel_new, conv_new, patch_grad = news
    return (
        block_out,
        patch_grad,
        qkv_grad,
        out_grad,
        norm_grad,
        bias_grad,
        kernel_grad,
        conv_grad,
        qkv_rows_new[0],
        qkv_cols_new[0],
        out_rows_new[0],
        out_cols_new[0],
        norm_second_new,
        bias_second_new,
        kernel_second_new,
        conv_second_new,
        qkv_new,
        out_new,
        norm_new,
        bias_new,
        kernel_new,
        conv_new,
    )


def solution(mesh):
    placed = (
        P(None, "head", "patch"),
        P(None, "patch"),
        P(),
        P(None, "head", "patch"),
        P("head", None),
        P("head", None),
        P(),
        P(None, "head"),
        P(None, "head"),
        P("head", None),
        P("head"),
        P(),
        P("head"),
        P(),
        P(),
        P(None, "head"),
        P(None, "head"),
        P("head", None),
    )
    return jax.shard_map(
        local,
        mesh=mesh,
        in_specs=placed,
        out_specs=(
            P(None, "head", "patch"),
            P(None, "head", "patch"),
            P("head", None),
            P("head", None),
            P(),
            P(None, "head"),
            P(None, "head"),
            P("head", None),
            P("head"),
            P(),
            P("head"),
            P(),
            P(),
            P(None, "head"),
            P(None, "head"),
            P("head", None),
            P("head", None),
            P("head", None),
            P(),
            P(None, "head"),
            P(None, "head"),
            P("head", None),
        ),
        check_vma=False,
    )
```

time: 978 us -> 259 us (0.26)
  waiting for transfers between devices: 396 us -> 58.7 us
  matrix products: 176 us -> 0 us
  other arithmetic: 139 us -> 5.14 us
  local copies, waits for them, and re-layouts: 115 us -> 24.4 us
  Pallas kernels: 28.4 us -> 108 us
  blocking collectives: 74.2 us -> 0 us
  starting transfers between devices: 11.3 us -> 42.7 us
  between operations: 29.1 us -> 15.3 us
    psum x5 -> x0, waiting for transfers between devices: 220 us -> none  [the longest x2 84.4 us: local(): query_sum, key_sum, counts = lax.psum((query_sum, key_sum, counts), 'patch')]
    dot_general x90 -> x0, matrix products: 167 us -> none  [the longest x69 119 us: matmul(): return jnp.matmul(left_side, right_side, precision=HIGHEST)]
    reduce_scatter x2 -> x1, waiting for transfers between devices: 141 us -> 0.01 us  [local(): lax.psum_scatter(grad_normed, 'head', scatter_dimension=0, tiled=True)[0]]
    pallas_call x0 -> x40, Pallas kernels: none -> 108 us  [the longest x2 9.89 us: grid_mix(): call(kernel, jax.ShapeDtypeStruct(own.shape, BF16), 1, room=GRID_ROOM, gr...]
    psum x4 -> x0, blocking collectives: 74.2 us -> none  [the longest x1 25.1 us: local(): lax.psum((qkv_grad, out_grad, norm_grad, bias_grad, kernel_grad, conv_gra...]
    reduce_sum x35 -> x0, other arithmetic: 57.1 us -> none  [the longest x3 17.2 us: local(): jnp.sum(grid_back * framed[0, :, :, row_shift:row_shift + grid_rows, col_...]
    convert_element_type x10 -> x7, other arithmetic: 42 us -> 1.85 us  [the longest x1 0.97 us: local(): out_low = out_weight.astype(BF16)]
    ppermute x6 -> x40, starting transfers between devices: 10.3 us -> 42.4 us  [the longest x33 32 us: swap_bits(): return lax.ppermute(value, axis, [(i, i ^ bits) for i in range(count)])]
  transfers between devices with their start and end apart: 16 -> 44, of which waited for: 10 -> 18; matrix products, arithmetic and copies ran while one was open for 22% -> 4% of each run, Pallas kernels for 3% -> 40%
where the time goes in v1:
time: 259 us; the launch traced here: 254 us
  Pallas kernels  108 us (42%)
  waiting for transfers between devices  58.7 us (23%)
  starting transfers between devices  42.7 us (16%)
  local copies, waits for them, and re-layouts  24.4 us (9%)
  between operations  15.3 us (6%)
  other arithmetic  5.14 us (2%)
    ppermute x33, starting transfers between devices, swap_bits(): return lax.ppermute(value, axis, [(i, i ^ bits) for i in range(count)])  32 us
    ppermute x33, waiting for transfers between devices, swap_bits(): return lax.ppermute(value, axis, [(i, i ^ bits) for i in range(count)])  29.3 us
    all_gather x1, waiting for transfers between devices, local(): gathered = lax.all_gather(patches, 'head')  28.6 us
    unnamed x126, local copies, waits for them, and re-layouts  18.1 us
    pallas_call x2, Pallas kernels, grid_mix(): call(kernel, jax.ShapeDtypeStruct(own.shape, BF16), 1, room=GRID_ROOM, gr...  9.89 us
    pallas_call x1, Pallas kernels, grid_back(): call(ordered(back_kernel, 1, 6), (jax.ShapeDtypeStruct(own.shape, F32), j...  8.97 us
    pallas_call x1, Pallas kernels, norm_project(): call(ordered(norm_kernel, len(after), 6 + len(after)), (jax.ShapeDtypeStr...  8.93 us
    pallas_call x1, Pallas kernels, landmark_pull(): call(ordered(pull_early_kernel, len(later), 7 + len(later)), jax.ShapeDty...  7.04 us
  transfers between devices with their start and end apart: 44, of which 18 were waited for; matrix products, arithmetic and copies ran while one was open for 4% of the time, Pallas kernels for 40%

profile of v1, /device:TPU:0, one launch (start us, length us, event | category | flops | bytes accessed | tf_op | source)
XLA Modules:
  0.0 254.0 jit_solution(1545581132342997669)
XLA Ops:
  9.1 3.1 %collective-permute-start.2 = (bf16[128,128]{1,0:T(8,128)(2,1)S(1)}, bf16[128,128]{1,0:T(8,128)(2,1)S(1)}, u32[]{:S(2)}, u32[]{:S(2)}) collective-permute-start(bf16[128,128]{1,0:T(8,128)(2,1)S(1)} %get-tuple-element.195), channel_id=1, source_target_pairs={{0,1},{1,2},{2,3},{3,0},{4,5},{5,6},{6,7},{7,4},{8,9},{9,10},{10,1... | collective-permute-start | bytes 98312 | tf_op jit(solution)/shard_map/ppermute | solution.py:1458
  20.7 9.0 %shard_map.345 = (f32[2,128,1152]{2,1,0:T(8,128)S(1)}, bf16[2,128,1152]{2,1,0:T(8,128)(2,1)}, f32[8,128]{1,0:T(8,128)S(1)}) custom-call(s32[5]{0:T(128)S(1)} %stack.70.refs_0_.refs_3_.scalars_ref, bf16[2,128,288]{2,1,0:T(8,128)(2,1)S(1)} %collective-permute-done.refs_1_, bf16[2,128,1152]{2,1,0:T(8,128)(2,1)S(1)} %copy-done.19, ...), custom_call_target="tpu_custom_call" | custom-call | flops 8000000000 | bytes 1024 | tf_op jit(solution)/shard_map/pallas_call | solution.py:597
  34.2 28.6 %all-gather.7.cloned.1.call-done = bf16[8,128,1152]{2,1,0:T(8,128)(2,1)} async-done(((bf16[2,128,1152]{2,1,0:T(8,128)(2,1)}), bf16[8,128,1152]{2,1,0:T(8,128)(2,1)}) %all-gather.7.cloned.1.call-update) | async-done | bytes 2359312 | tf_op jit(solution)/shard_map/all_gather | solution.py:1449
  62.8 8.9 %shard_map.347 = (bf16[2,512,1152]{2,1,0:T(8,128)(2,1)}, f32[2,8,1152]{2,1,0:T(8,128)}, bf16[2,2,192,1152]{3,2,1,0:T(8,128)(2,1)}, f32[2,136,256]{2,1,0:T(8,128)}, f32[2,136,256]{2,1,0:T(8,128)}) custom-call(s32[5]{0:T(128)} %copy-done.27, bf16[4,2,128,1152]{3,2,1,0:T(8,128)(2,1)} %bitcast.54, bf16[384,512]{1,0:T(8,128)(2,1)} %convert_element_type.46.refs_2_.weight_ref, ...), custom_call_target="tpu_custom_call" | custom-call | flops 100000000 | bytes 1024 | tf_op jit(solution)/shard_map/pallas_call | solution.py:850
  92.3 3.2 %shard_map.352 = (bf16[2,2,256,1152]{3,2,1,0:T(8,128)(2,1)S(1)}, f32[2,72,256]{2,1,0:T(8,128)S(1)}, f32[2,72,256]{2,1,0:T(8,128)S(1)}) custom-call(s32[5]{0:T(128)S(1)} %copy-done.28, bf16[2,2,192,1152]{3,2,1,0:T(8,128)(2,1)S(1)} %copy-done, bf16[2,2,128,256]{3,2,1,0:T(8,128)(2,1)S(1)} %pad_maximum_fusion.2.refs_2_.refs_1_, s32[2,1152]{1,0:T(2,128)S(1)} %copy-done.32, ...), custom_call_target="tpu_custom_call" | custom-call | flops 100000000 | bytes 1024 | tf_op jit(solution)/shard_map/pallas_call | solution.py:1015
  100.6 4.8 %shard_map.354 = (f32[256,256]{1,0:T(8,128)}, f32[3,256,256]{2,1,0:T(8,128)}, f32[3,256,256]{2,1,0:T(8,128)}, f32[2,256,256]{2,1,0:T(8,128)}, f32[8,128]{1,0:T(8,128)}) custom-call(bf16[128,256]{1,0:T(8,128)(2,1)} %copy-done.18, f32[2,72,256]{2,1,0:T(8,128)} %copy-done.45), custom_call_target="tpu_custom_call" | custom-call | flops 100000000 | bytes 1024 | tf_op jit(solution)/shard_map/pallas_call | solution.py:313
  107.3 4.1 %shard_map.356 = (f32[256,256]{1,0:T(8,128)}, f32[3,256,256]{2,1,0:T(8,128)}, f32[3,256,256]{2,1,0:T(8,128)}) custom-call(f32[2,256,256]{2,1,0:T(8,128)} %get-tuple-element.106.refs_0_, bf16[128,256]{1,0:T(8,128)(2,1)} %copy-done.18), custom_call_target="tpu_custom_call" | custom-call | flops 100000000 | bytes 1024 | tf_op jit(solution)/shard_map/pallas_call | solution.py:331
  117.3 5.3 %shard_map.359 = (bf16[2,2,64,1152]{3,2,1,0:T(8,128)(2,1)}, f32[2,64,256]{2,1,0:T(8,128)}, f32[2,64,256]{2,1,0:T(8,128)}) custom-call(s32[5]{0:T(128)} %copy-done.27, bf16[4,2,128,1152]{3,2,1,0:T(8,128)(2,1)} %bitcast.52, bf16[128,512]{1,0:T(8,128)(2,1)} %copy-done.60, bf16[2,2,256,1152]{3,2,1,0:T(8,128)(2,1)} %copy-done.1, f32[72,256]{1,0:T(8,128)} %copy-done.11), custom_call_target="tpu_custom_call" | custom-call | flops 100000000 | bytes 1024 | tf_op jit(solution)/shard_map/pallas_call | solution.py:913
  135.8 3.9 %shard_map.364 = (bf16[2,2,64,1152]{3,2,1,0:T(8,128)(2,1)S(1)}, f32[2,2,64,256]{3,2,1,0:T(8,128)S(1)}) custom-call(bf16[2,2,192,1152]{3,2,1,0:T(8,128)(2,1)S(1)} %copy-done, bf16[2,2,128,256]{3,2,1,0:T(8,128)(2,1)S(1)} %pad_maximum_fusion.2.refs_2_.refs_1_, bf16[2,2,64,256]{3,2,1,0:T(8,128)(2,1)S(1)} %pad_maximum_fusion.9.refs_0_.refs_2_, ...), custom_call_target="tpu_custom_call" | custom-call | flops 1000000000 | bytes 1024 | tf_op jit(solution)/shard_map/pallas_call | solution.py:1035
  140.7 4.0 %shard_map.367 = (f32[13,64,256]{2,1,0:T(8,128)}, f32[8,128]{1,0:T(8,128)}) custom-call(f32[72,256]{1,0:T(8,128)} %copy-done.11, f32[64,256]{1,0:T(8,128)} %copy-done.22, f32[256,256]{1,0:T(8,128)} %get-tuple-element.117.kernel_ref.refs_3_, f32[3,256,256]{2,1,0:T(8,128)} %get-tuple-element.118.early_ref.refs_4_, ...), custom_call_target="tpu_custom_call" | custom-call | flops 1000000000 | bytes 1024 | tf_op jit(solution)/shard_map/pallas_call | solution.py:360
  147.4 4.0 %shard_map.369 = (bf16[2,2,64,1152]{3,2,1,0:T(8,128)(2,1)S(1)}, bf16[2,2,64,1152]{3,2,1,0:T(8,128)(2,1)S(1)}, f32[2,128,256]{2,1,0:T(8,128)S(1)}, f32[2,128,256]{2,1,0:T(8,128)}) custom-call(s32[5]{0:T(128)S(1)} %copy-done.29, bf16[2,2,192,1152]{3,2,1,0:T(8,128)(2,1)S(1)} %copy-done, bf16[2,2,128,256]{3,2,1,0:T(8,128)(2,1)S(1)} %pad_maximum_fusion.2.refs_2_.refs_1_, ...), custom_call_target="tpu_custom_call" | custom-call | flops 1000000000 | bytes 1024 | tf_op jit(solution)/shard_map/pallas_call | solution.py:1050
  158.4 6.0 %shard_map.371.refs_0_ = f32[256,256]{1,0:T(8,128)} custom-call(f32[13,64,256]{2,1,0:T(8,128)} %get-tuple-element.127.refs_0_.refs_6_, f32[3,256,256]{2,1,0:T(8,128)} %get-tuple-element.119.late_ref.refs_1_, f32[3,256,256]{2,1,0:T(8,128)} %get-tuple-element.128.refs_2_, f32[2,128,256]{2,1,0:T(8,128)} %copy-done.21), custom_call_target="tpu_custom_call" | custom-call | flops 2000000000 | bytes 1024 | tf_op jit(solution)/shard_map/pallas_call | solution.py:373
  166.9 7.0 %shard_map.372.refs_1_ = f32[128,256]{1,0:T(8,128)} custom-call(f32[256,256]{1,0:T(8,128)} %shard_map.371.refs_0_, bf16[128,256]{1,0:T(8,128)(2,1)} %copy-done.18, f32[64,256]{1,0:T(8,128)} %copy-done.22, f32[256,256]{1,0:T(8,128)} %get-tuple-element.117.kernel_ref.refs_3_, f32[3,256,256]{2,1,0:T(8,128)} %get-tuple-element.118.early_ref.refs_4_, ...), custom_call_target="tpu_custom_call" | custom-call | flops 2000000000 | bytes 1024 | tf_op jit(solution)/shard_map/pallas_call | solution.py:380
  178.3 3.9 %shard_map.374 = (bf16[2,2,64,1152]{3,2,1,0:T(8,128)(2,1)S(1)}, f32[2,40,128]{2,1,0:T(8,128)S(1)}) custom-call(s32[5]{0:T(128)S(1)} %copy-done.29, bf16[2,2,64,16]{3,2,1,0:T(8,128)(2,1)S(1)} %collective-permute-done.9.refs_4_.inner_ref.refs_1_, bf16[2,2,192,1152]{3,2,1,0:T(8,128)(2,1)S(1)} %copy-done, ...), custom_call_target="tpu_custom_call" | custom-call | flops 1000000000 | bytes 1024 | tf_op jit(solution)/shard_map/pallas_call | solution.py:783
  184.4 6.7 %shard_map.376 = (bf16[4,2,128,1152]{3,2,1,0:T(8,128)(2,1)S(1)}, f32[2,2,1152]{2,1,0:T(2,128)S(1)}, f32[8,512]{1,0:T(8,128)S(1)}, f32[256,512]{1,0:T(8,128)S(1)}, bf16[256,512]{1,0:T(8,128)(2,1)S(1)}) custom-call(s32[5]{0:T(128)S(1)} %copy-done.29, bf16[2,2,64,1152]{3,2,1,0:T(8,128)(2,1)S(1)} %copy-done.51, bf16[2,2,64,1152]{3,2,1,0:T(8,128)(2,1)S(1)} %copy-done.53, ...), custom_call_target="tpu_custom_call" | custom-call | flops 7000000000 | bytes 1024 | tf_op jit(solution)/shard_map/pallas_call | solution.py:1113
  197.5 3.3 %collective-permute-start.33 = (bf16[128,512]{1,0:T(8,128)(2,1)S(1)}, bf16[128,512]{1,0:T(8,128)(2,1)S(1)}, u32[]{:S(2)}, u32[]{:S(2)}) collective-permute-start(bf16[128,512]{1,0:T(8,128)(2,1)S(1)} %get-tuple-element.137), channel_id=1, source_target_pairs={{0,8},{4,12},{8,0},{12,4},{16,24},{20,28},{24,16},{28,20},{1,9},{5... | collective-permute-start | bytes 393224 | tf_op jit(solution)/shard_map/ppermute | solution.py:42
  200.9 3.3 %shard_map.378.refs_3_.held_ref = f32[49,8,128]{2,1,0:T(8,128)S(1)} custom-call(s32[5]{0:T(128)S(1)} %copy-done.29, bf16[2,128,288]{2,1,0:T(8,128)(2,1)S(1)} %collective-permute-done.18.inner_ref.refs_1_, f32[2,128,1152]{2,1,0:T(8,128)S(1)} %shard_map.361.own_ref.refs_2_.refs_3_, bf16[2,128,288]{2,1,0:T(8,128)(2,1)S(1)} %collective-permute-done.19.outer_ref.refs_3_, ...), custom_call_target="tpu_custom_call" | custom-call | flops 1000000000 | bytes 1024 | tf_op jit(solution)/shard_map/pallas_call | solution.py:627
  204.2 3.6 %collective-permute-done.33.refs_2_ = bf16[128,512]{1,0:T(8,128)(2,1)S(1)} collective-permute-done((bf16[128,512]{1,0:T(8,128)(2,1)S(1)}, bf16[128,512]{1,0:T(8,128)(2,1)S(1)}, u32[]{:S(2)}, u32[]{:S(2)}) %collective-permute-start.33) | collective-permute-done | bytes 131104 | tf_op jit(solution)/shard_map/ppermute | solution.py:42
  209.9 3.5 %shard_map.380.sums_ref = f32[49,8,128]{2,1,0:T(8,128)S(1)} custom-call(s32[5]{0:T(128)S(1)} %copy-done.29, bf16[2,128,288]{2,1,0:T(8,128)(2,1)S(1)} %collective-permute-done.18.inner_ref.refs_1_, f32[2,128,1152]{2,1,0:T(8,128)S(1)} %shard_map.361.own_ref.refs_2_.refs_3_, bf16[2,128,288]{2,1,0:T(8,128)(2,1)S(1)} %collective-permute-done.19.outer_ref.refs_3_, ...), custom_call_target="tpu_custom_call" | custom-call | flops 1000000000 | bytes 1024 | tf_op jit(solution)/shard_map/pallas_call | solution.py:627
  214.5 3.8 %collective-permute-done.35 = bf16[80,512]{1,0:T(8,128)(2,1)S(1)} collective-permute-done((bf16[80,512]{1,0:T(8,128)(2,1)S(1)}, bf16[80,512]{1,0:T(8,128)(2,1)S(1)}, u32[]{:S(2)}, u32[]{:S(2)}) %collective-permute-start.35) | collective-permute-done | bytes 81952 | tf_op jit(solution)/shard_map/ppermute | solution.py:42
  219.6 4.4 %collective-permute-done.36 = bf16[144,512]{1,0:T(8,128)(2,1)S(1)} collective-permute-done((bf16[144,512]{1,0:T(8,128)(2,1)S(1)}, bf16[144,512]{1,0:T(8,128)(2,1)S(1)}, u32[]{:S(2)}, u32[]{:S(2)}) %collective-permute-start.36) | collective-permute-done | bytes 147488 | tf_op jit(solution)/shard_map/ppermute | solution.py:42
  226.6 4.9 %shard_map.362.refs_6_ = bf16[2,128,1152]{2,1,0:T(8,128)(2,1)} custom-call(s32[5]{0:T(128)S(1)} %copy-done.29, bf16[2,128,288]{2,1,0:T(8,128)(2,1)S(1)} %collective-permute-done.18.inner_ref.refs_1_, f32[2,128,1152]{2,1,0:T(8,128)S(1)} %shard_map.361.own_ref.refs_2_.refs_3_, bf16[2,128,288]{2,1,0:T(8,128)(2,1)S(1)} %collective-permute-done.19.outer_ref.refs_3_, ...), custom_call_target="tpu_custom_call" | custom-call | flops 1000000000 | bytes 1024 | tf_op jit(solution)/shard_map/pallas_call | solution.py:647
  233.4 4.9 %shard_map.363 = bf16[2,128,1152]{2,1,0:T(8,128)(2,1)} custom-call(s32[5]{0:T(128)S(1)} %copy-done.29, bf16[2,128,288]{2,1,0:T(8,128)(2,1)S(1)} %collective-permute-done.18.inner_ref.refs_1_, f32[2,128,1152]{2,1,0:T(8,128)S(1)} %shard_map.361.own_ref.refs_2_.refs_3_, ...), custom_call_target="tpu_custom_call", output_to_operand_aliasing={{}: (6, {})} | custom-call | flops 1000000000 | bytes 1024 | tf_op jit(solution)/shard_map/pallas_call | solution.py:647
  242.6 4.6 %shard_map.384 = (f32[2,512]{1,0:T(2,128)}, f32[1,512]{1,0:T(1,128)}, f32[1,512]{1,0:T(1,128)}, f32[2,512]{1,0:T(2,128)}, f32[384,512]{1,0:T(8,128)}, /*index=5*...) custom-call(f32[24,512]{1,0:T(8,128)} %add.147.refs_0_, ...), custom_call_target="tpu_custom_call" | custom-call | flops 200000000 | bytes 1024 | tf_op jit(solution)/shard_map/pallas_call | solution.py:1399
  (295 shorter events, 99.7 us)
Async XLA Ops:
  7.2 55.6 %all-gather.7.cloned.1.call-start = ((), (), s32[]{:S(2)}) async-start(), calls=%async_computation.2 | async-start | bytes 2949120 | tf_op jit(solution)/shard_map/all_gather | solution.py:1449
  7.9 109.4 %all-gather.9.cloned.1.call-start = ((), (), s32[]{:S(2)}) async-start(), calls=%async_computation.3 | async-start | bytes 2949120 | tf_op jit(solution)/shard_map/all_gather | solution.py:1471
  9.1 11.4 %collective-permute-start.2 = (bf16[128,128]{1,0:T(8,128)(2,1)S(1)}, bf16[128,128]{1,0:T(8,128)(2,1)S(1)}, u32[]{:S(2)}, u32[]{:S(2)}) collective-permute-start(bf16[128,128]{1,0:T(8,128)(2,1)S(1)} %get-tuple-element.195), channel_id=1, source_target_pairs={{0,1},{1,2},{2,3},{3,0},{4,5},{5,6},{6,7},{7,4},{8,9},{9,10},{10,1... | collective-permute-start | bytes 98312 | tf_op jit(solution)/shard_map/ppermute | solution.py:1458
  12.2 8.4 %collective-permute-start.3 = (bf16[128,128]{1,0:T(8,128)(2,1)S(1)}, bf16[128,128]{1,0:T(8,128)(2,1)S(1)}, u32[]{:S(2)}, u32[]{:S(2)}) collective-permute-start(bf16[128,128]{1,0:T(8,128)(2,1)S(1)} %get-tuple-element.194), channel_id=1, source_target_pairs={{0,2},{1,3},{2,0},{3,1},{4,6},{5,7},{6,4},{7,5},{8,10},{9,11},{10,... | collective-permute-start | bytes 98312 | tf_op jit(solution)/shard_map/ppermute | solution.py:1458
  14.7 5.8 %collective-permute-start.4 = (bf16[128,128]{1,0:T(8,128)(2,1)S(1)}, bf16[128,128]{1,0:T(8,128)(2,1)S(1)}, u32[]{:S(2)}, u32[]{:S(2)}) collective-permute-start(bf16[128,128]{1,0:T(8,128)(2,1)S(1)} %get-tuple-element.193), channel_id=1, source_target_pairs={{0,3},{1,0},{2,1},{3,2},{4,7},{5,4},{6,5},{7,6},{8,11},{9,8},{10,9... | collective-permute-start | bytes 98312 | tf_op jit(solution)/shard_map/ppermute | solution.py:1458
  30.7 162.0 %all-gather.11.cloned.1.call-start = ((), (), s32[]{:S(2)}) async-start(), calls=%async_computation.4 | async-start | bytes 2949120 | tf_op jit(solution)/shard_map/all_gather | solution.py:1502
  75.1 9.8 %collective-permute-start.6 = (f32[136,256]{1,0:T(8,128)S(1)}, f32[136,256]{1,0:T(8,128)S(1)}, u32[]{:S(2)}, u32[]{:S(2)}) collective-permute-start(f32[136,256]{1,0:T(8,128)S(1)} %get-tuple-element.98.refs_0_), channel_id=1, source_target_pairs={{0,16},{4,20},{8,24},{12,28},{16,0},{20,4},{24,8},{28,12},{1,17},{... | collective-permute-start | bytes 417800 | tf_op jit(solution)/shard_map/ppermute | solution.py:42
  76.7 8.2 %collective-permute-start.7 = (f32[136,256]{1,0:T(8,128)S(1)}, f32[136,256]{1,0:T(8,128)S(1)}, u32[]{:S(2)}, u32[]{:S(2)}) collective-permute-start(f32[136,256]{1,0:T(8,128)S(1)} %get-tuple-element.99), channel_id=1, source_target_pairs={{0,8},{4,12},{8,0},{12,4},{16,24},{20,28},{24,16},{28,20},{1,9},{5... | collective-permute-start | bytes 417800 | tf_op jit(solution)/shard_map/ppermute | solution.py:42
  78.2 6.9 %collective-permute-start.8 = (f32[136,256]{1,0:T(8,128)S(1)}, f32[136,256]{1,0:T(8,128)S(1)}, u32[]{:S(2)}, u32[]{:S(2)}) collective-permute-start(f32[136,256]{1,0:T(8,128)S(1)} %get-tuple-element.99), channel_id=1, source_target_pairs={{0,24},{4,28},{8,16},{12,20},{16,8},{20,12},{24,0},{28,4},{1,25},{... | collective-permute-start | bytes 417800 | tf_op jit(solution)/shard_map/ppermute | solution.py:42
  98.8 6.6 %collective-permute-start.14 = (f32[72,256]{1,0:T(8,128)S(1)}, f32[72,256]{1,0:T(8,128)S(1)}, u32[]{:S(2)}, u32[]{:S(2)}) collective-permute-start(f32[72,256]{1,0:T(8,128)S(1)} %get-tuple-element.104), channel_id=1, source_target_pairs={{0,8},{4,12},{8,0},{12,4},{16,24},{20,28},{24,16},{28,20},{1,9},{5... | collective-permute-start | bytes 221192 | tf_op jit(solution)/shard_map/ppermute | solution.py:42
  106.1 5.3 %collective-permute-start.15 = (f32[72,256]{1,0:T(8,128)S(1)}, f32[72,256]{1,0:T(8,128)S(1)}, u32[]{:S(2)}, u32[]{:S(2)}) collective-permute-start(f32[72,256]{1,0:T(8,128)S(1)} %shard_map.355), channel_id=1, source_target_pairs={{0,16},{4,20},{8,24},{12,28},{16,0},{20,4},{24,8},{28,12},{1,17},{... | collective-permute-start | bytes 221192 | tf_op jit(solution)/shard_map/ppermute | solution.py:42
  117.2 5.5 %collective-permute-start.17 = (bf16[2,64,256]{2,1,0:T(8,128)(2,1)S(1)}, bf16[2,64,256]{2,1,0:T(8,128)(2,1)}, u32[]{:S(2)}, u32[]{:S(2)}) collective-permute-start(bf16[2,64,256]{2,1,0:T(8,128)(2,1)S(1)} %shard_map.358), channel_id=1, source_target_pairs={{0,4},{4,0},{8,12},{12,8},{16,20},{20,16},{24,28},{28,24},{1,5},{5... | collective-permute-start | bytes 196616 | tf_op jit(solution)/shard_map/ppermute | solution.py:42
  125.8 116.7 %reduce-scatter.2.cloned.1.call-start = ((), (), s32[]{:S(2)}) async-start(), calls=%async_computation.1 | async-start | bytes 2949120 | tf_op jit(solution)/shard_map/reduce_scatter | solution.py:1542
  133.7 6.0 %collective-permute-start.22 = (f32[64,256]{1,0:T(8,128)S(1)}, f32[64,256]{1,0:T(8,128)S(1)}, u32[]{:S(2)}, u32[]{:S(2)}) collective-permute-start(f32[64,256]{1,0:T(8,128)S(1)} %add.138), channel_id=1, source_target_pairs={{0,16},{4,20},{8,24},{12,28},{16,0},{20,4},{24,8},{28,12},{1,17},{... | collective-permute-start | bytes 196616 | tf_op jit(solution)/shard_map/ppermute | solution.py:42
  153.4 12.8 %collective-permute-start.25 = (bf16[2,2,64,16]{3,2,1,0:T(8,128)(2,1)S(1)}, bf16[2,2,64,16]{3,2,1,0:T(8,128)(2,1)S(1)}, u32[]{:S(2)}, u32[]{:S(2)}) collective-permute-start(bf16[2,2,64,16]{3,2,1,0:T(8,128)(2,1)S(1)} %get-tuple-element.169), channel_id=1, source_target_pairs={{0,4},{4,0},{8,12},{12,8},{16,20},{20,16},{24,28},{28,24},{1,5},{5... | collective-permute-start | bytes 24584 | tf_op jit(solution)/shard_map/ppermute | solution.py:42
  153.8 12.4 %collective-permute-start.26 = (bf16[2,2,64,16]{3,2,1,0:T(8,128)(2,1)S(1)}, bf16[2,2,64,16]{3,2,1,0:T(8,128)(2,1)S(1)}, u32[]{:S(2)}, u32[]{:S(2)}) collective-permute-start(bf16[2,2,64,16]{3,2,1,0:T(8,128)(2,1)S(1)} %get-tuple-element.168), channel_id=1, source_target_pairs={{4,8},{12,16},{20,24},{8,4},{16,12},{24,20},{5,9},{13,17},{21,25},... | collective-permute-start | bytes 24584 | tf_op jit(solution)/shard_map/ppermute | solution.py:125
  155.3 9.0 %collective-permute-start.28 = (f32[128,256]{1,0:T(8,128)S(1)}, f32[128,256]{1,0:T(8,128)S(1)}, u32[]{:S(2)}, u32[]{:S(2)}) collective-permute-start(f32[128,256]{1,0:T(8,128)S(1)} %get-tuple-element.126), channel_id=1, source_target_pairs={{0,8},{4,12},{8,0},{12,4},{16,24},{20,28},{24,16},{28,20},{1,9},{5... | collective-permute-start | bytes 393224 | tf_op jit(solution)/shard_map/ppermute | solution.py:42
  164.4 9.6 %collective-permute-start.29 = (f32[128,256]{1,0:T(8,128)S(1)}, f32[128,256]{1,0:T(8,128)S(1)}, u32[]{:S(2)}, u32[]{:S(2)}) collective-permute-start(f32[128,256]{1,0:T(8,128)S(1)} %add.140), channel_id=1, source_target_pairs={{0,16},{4,20},{8,24},{12,28},{16,0},{20,4},{24,8},{28,12},{1,17},{... | collective-permute-start | bytes 393224 | tf_op jit(solution)/shard_map/ppermute | solution.py:42
  175.0 7.2 %collective-permute-start.30 = (bf16[128,256]{1,0:T(8,128)(2,1)S(1)}, bf16[128,256]{1,0:T(8,128)(2,1)S(1)}, u32[]{:S(2)}, u32[]{:S(2)}) collective-permute-start(bf16[128,256]{1,0:T(8,128)(2,1)S(1)} %shard_map.373.refs_8_.refs_1_), channel_id=1, source_target_pairs={{0,8},{4,12},{8,0},{12,4},{16,24},{20,28},{24,16},{28,20},{1,9},{5... | collective-permute-start | bytes 196616 | tf_op jit(solution)/shard_map/ppermute | solution.py:42
  197.5 10.3 %collective-permute-start.33 = (bf16[128,512]{1,0:T(8,128)(2,1)S(1)}, bf16[128,512]{1,0:T(8,128)(2,1)S(1)}, u32[]{:S(2)}, u32[]{:S(2)}) collective-permute-start(bf16[128,512]{1,0:T(8,128)(2,1)S(1)} %get-tuple-element.137), channel_id=1, source_target_pairs={{0,8},{4,12},{8,0},{12,4},{16,24},{20,28},{24,16},{28,20},{1,9},{5... | collective-permute-start | bytes 393224 | tf_op jit(solution)/shard_map/ppermute | solution.py:42
  208.4 5.2 %collective-permute-start.34 = (bf16[64,512]{1,0:T(8,128)(2,1)S(1)}, bf16[64,512]{1,0:T(8,128)(2,1)S(1)}, u32[]{:S(2)}, u32[]{:S(2)}) collective-permute-start(bf16[64,512]{1,0:T(8,128)(2,1)S(1)} %get-tuple-element.139), channel_id=1, source_target_pairs={{0,16},{4,20},{8,24},{12,28},{16,0},{20,4},{24,8},{28,12},{1,17},{... | collective-permute-start | bytes 196616 | tf_op jit(solution)/shard_map/ppermute | solution.py:42
  218.4 5.7 %collective-permute-start.36 = (bf16[144,512]{1,0:T(8,128)(2,1)S(1)}, bf16[144,512]{1,0:T(8,128)(2,1)S(1)}, u32[]{:S(2)}, u32[]{:S(2)}) collective-permute-start(bf16[144,512]{1,0:T(8,128)(2,1)S(1)} %pad_maximum_fusion.6), channel_id=1, source_target_pairs={{0,8},{4,12},{8,0},{12,4},{16,24},{20,28},{24,16},{28,20},{1,9},{5... | collective-permute-start | bytes 442376 | tf_op jit(solution)/shard_map/ppermute | solution.py:42
  226.5 6.3 %collective-permute-start.38 = (f32[24,512]{1,0:T(8,128)S(1)}, f32[24,512]{1,0:T(8,128)S(1)}, u32[]{:S(2)}, u32[]{:S(2)}) collective-permute-start(f32[24,512]{1,0:T(8,128)S(1)} %shard_map.382.refs_7_), channel_id=1, source_target_pairs={{0,1},{1,0},{2,3},{3,2},{4,5},{5,4},{6,7},{7,6},{8,9},{9,8},{10,11... | collective-permute-start | bytes 147464 | tf_op jit(solution)/shard_map/ppermute | solution.py:42
  232.8 9.2 %collective-permute-start.39 = (f32[24,512]{1,0:T(8,128)S(1)}, f32[24,512]{1,0:T(8,128)S(1)}, u32[]{:S(2)}, u32[]{:S(2)}) collective-permute-start(f32[24,512]{1,0:T(8,128)S(1)} %add.146), channel_id=1, source_target_pairs={{0,2},{1,3},{2,0},{3,1},{4,6},{5,7},{6,4},{7,5},{8,10},{9,11},{10,... | collective-permute-start | bytes 147464 | tf_op jit(solution)/shard_map/ppermute | solution.py:42
  (83 other events, 531.5 us)
Sparse Core Ops, SparseCore 0:
  9.6 53.1 all-gather.6
  65.0 49.2 all-gather.8
  125.9 48.4 all-gather.10
  192.6 47.5 reduce-scatter.1
